TPU v7x, 768 devices: a whole 4x8x12 slice. The times are simulated.
768 devices in a mesh: sec: 4 (over y_lo), sp: 8 (over x, core), dp: 24 (over y_hi, z).
Axes of the slice: x: 4, y: 8 (y_hi: 2, y_lo: 4; y = y_hi * 4 + y_lo), z: 12, core: 2. Of those that a mesh axis runs over, the one named last changes fastest.
Arguments:
- fraction: float32 [24, 32, 32, 1024], P('dp', None, 'sp', 'sec'), may hold values from 0 to 1
- labels: int32 [24, 32, 32, 1024], P('dp', ('sec', 'sp')), may hold values from 0 to 63
- conv_weight: bfloat16 [54, 64], replicated, may hold values from -6 to 6
- conv_bias: float32 [64], replicated, may hold values from -6 to 6
- out_weight: bfloat16 [64, 64], replicated, may hold values from -6 to 6
- out_bias: float32 [64], replicated, may hold values from -6 to 6
Outputs:
- cell_loss: float32 [24, 32, 32, 1024], P('dp', ('sec', 'sp'))
- conv_weight_grad: float32 [54, 64], replicated
- conv_bias_grad: float32 [64], replicated
- out_weight_grad: float32 [64, 64], replicated
- out_bias_grad: float32 [64], replicated
All inputs are finite; a program needn't handle non-finite values.
Results may differ from a plain program's by a relative error of at most 0.00035.
The roundings to bfloat16 on the way count: a program that leaves them out, or rounds other values in their place, can miss the bound.
Values may be sent and summed in bfloat16 or wider, within the bound.
A program may use at most 32 MiB of HBM per device.

v0:
```python
import jax
import jax.numpy as jnp
from jax import lax
from jax.sharding import PartitionSpec as P

PY = 32
PZ = 32


def extended(cells, sides, width):
    for axis, dim in sides:
        count = lax.axis_size(axis)
        ends = count - 1
        head = lax.slice_in_dim(cells, 0, width, axis=dim)
        tail = lax.slice_in_dim(cells, cells.shape[dim] - width, cells.shape[dim], axis=dim)
        cells = jnp.concatenate(
            [
                lax.ppermute(tail, axis, [(i, (i + 1) % count) for i in range(ends)]),
                cells,
                lax.ppermute(head, axis, [((i + 1) % count, i) for i in range(ends)]),
            ],
            axis=dim,
        )
    return cells


def shift_cells(values, offset, step_y, step_z):
    length = values.shape[-1]
    margin = PY * PZ + PZ + 1
    widths = [(0, 0)] * (values.ndim - 1) + [(margin, margin)]
    padded = jnp.pad(values, widths)
    shifted = lax.slice_in_dim(
        padded, margin + offset, margin + offset + length, axis=values.ndim - 1
    )
    position = jnp.arange(length, dtype=jnp.int32)
    row_y = position // PZ % PY + step_y
    col_z = position % PZ + step_z
    inside = (row_y >= 0) & (row_y < PY) & (col_z >= 0) & (col_z < PZ)
    return jnp.where(inside, shifted, jnp.zeros((), values.dtype))


def brick_box(rimmed):
    x_sums = rimmed[:, :-2] + rimmed[:, 1:-1] + rimmed[:, 2:]
    y_sums = x_sums[:, :, :-2] + x_sums[:, :, 1:-1] + x_sums[:, :, 2:]
    z_padded = jnp.pad(y_sums, ((0, 0), (0, 0), (0, 0), (1, 1)))
    z_sums = z_padded[..., :-2] + z_padded[..., 1:-1] + z_padded[..., 2:]
    return z_sums / 27.0


def joint_layout(arrived, sections):
    channels, patches, planes, width = arrived.shape
    split = arrived.reshape(channels, patches, sections, planes // sections, width)
    ordered = split.transpose(0, 1, 3, 2, 4)
    return ordered.reshape(channels, patches, planes // sections, sections * width)


def relay_features(block):
    arrived = lax.all_to_all(block, ("sec", "sp"), split_axis=1, concat_axis=2, tiled=True)
    result = joint_layout(arrived, lax.axis_size("sec"))
    return result


def make_columns(features):
    shifted_list = []
    for step_x in (-1, 0, 1):
        for step_y in (-1, 0, 1):
            for step_z in (-1, 0, 1):
                offset = step_x * PY * PZ + step_y * PZ + step_z
                shifted_list.append(shift_cells(features, offset, step_y, step_z))
    stacked = jnp.stack(shifted_list)
    return stacked.reshape(2 * stacked.shape[0], stacked.shape[2])


def patch_step(features, patch_labels, conv_weight, conv_bias, out_weight, out_bias, weight_scale):
    columns = make_columns(features)
    hidden_pre = (
        jnp.einsum("kc,kh->hc", columns, conv_weight, preferred_element_type=jnp.float32)
        + conv_bias[:, None]
    )
    hidden_act = jax.nn.silu(hidden_pre).astype(jnp.bfloat16)
    logits = (
        jnp.einsum("hb,hc->bc", out_weight, hidden_act, preferred_element_type=jnp.float32)
        + out_bias[:, None]
    )
    exp_logits = jnp.exp(logits)
    partition = jnp.sum(exp_logits, axis=0)
    bin_ids = jnp.arange(logits.shape[0], dtype=jnp.int32)[:, None]
    is_label = bin_ids == patch_labels[None, :]
    cell_term = jnp.log(partition) - jnp.sum(jnp.where(is_label, logits, 0.0), axis=0)
    residual = (exp_logits / partition - is_label.astype(jnp.float32)) * weight_scale
    residual_low = residual.astype(jnp.bfloat16)
    out_weight_grad = jnp.einsum(
        "hc,bc->hb", hidden_act, residual_low, preferred_element_type=jnp.float32
    )
    out_bias_grad = jnp.sum(residual, axis=1)
    hidden_back = jnp.einsum(
        "hb,bc->hc", out_weight, residual_low, preferred_element_type=jnp.float32
    )
    sigmoid_pre = jax.nn.sigmoid(hidden_pre)
    hidden_grad = hidden_back * sigmoid_pre * (1.0 + hidden_pre * (1.0 - sigmoid_pre))
    conv_bias_grad = jnp.sum(hidden_grad, axis=1)
    hidden_low = hidden_grad.astype(jnp.bfloat16)
    conv_weight_grad = jnp.einsum(
        "kc,hc->kh", columns, hidden_low, preferred_element_type=jnp.float32
    )
    return (cell_term, (conv_weight_grad, conv_bias_grad, out_weight_grad, out_bias_grad))


def shards(fraction, labels, conv_weight, conv_bias, out_weight, out_bias):
    brick = fraction[0]
    patch_total, plane_count, row_width = brick.shape
    cubic = brick.reshape(patch_total, plane_count, row_width // PZ, PZ)
    rimmed = extended(cubic, (("sec", 2), ("sp", 1)), 1)
    filt = brick_box(rimmed)
    filt_sq = brick_box(rimmed * rimmed)
    local_feats = jnp.stack([filt, filt_sq - filt * filt]).astype(jnp.bfloat16)
    local_feats = local_feats.reshape(2, patch_total, plane_count, row_width)
    arrived = relay_features(local_feats)
    features = arrived.transpose(1, 0, 2, 3)
    patch_count = features.shape[0]
    features = features.reshape(patch_count, 2, -1)
    flat_labels = labels[0].reshape(patch_count, -1)
    cell_count = flat_labels.shape[1]
    weight_scale = 1.0 / (
        lax.axis_size("sec") * lax.axis_size("sp") * lax.axis_size("dp") * patch_count * cell_count
    )
    cell_term, terms = patch_step(
        features[0], flat_labels[0], conv_weight, conv_bias, out_weight, out_bias, weight_scale
    )
    conv_wsum = terms[0]
    conv_bsum = terms[1]
    out_wsum = terms[2]
    out_bsum = terms[3]
    losses = [cell_term]
    summed = lax.psum((conv_wsum, conv_bsum, out_wsum, out_bsum), ("sec", "sp", "dp"))
    cell_loss = jnp.stack(losses).reshape(labels.shape)
    return (cell_loss, summed[0], summed[1], summed[2], summed[3])


def solution(mesh):
    placed = (P("dp", None, "sp", "sec"), P("dp", ("sec", "sp"), None, None), P(), P(), P(), P())
    return jax.shard_map(
        shards,
        mesh=mesh,
        in_specs=placed,
        out_specs=(P("dp", ("sec", "sp"), None, None), P(), P(), P(), P()),
        check_vma=False,
    )
```

profile of v0, /device:TPU:1, one launch (start us, length us, event | category | flops | bytes accessed | tf_op | source)
XLA Modules:
  0.0 220.6 jit_solution(12184737374747031123)
XLA Ops:
  0.6 0.0 copy-start
  0.7 1.1 reshape_squeeze.3
  1.8 0.1 fusion.83
  1.9 4.0 %collective-permute-start = (f32[32,4,1,32]{3,2,0,1:T(1,128)S(1)}, f32[32,4,1,32]{3,2,0,1:T(1,128)S(1)}, u32[]{:S(2)}, u32[]{:S(2)}) collective-permute-start(f32[32,4,1,32]{3,2,0,1:T(1,128)S(1)} %get-tuple-element.15), channel_id=1, source_target_pairs={{0,192},{192,384},{384,576},{1,193},{193,385},{385,577},{2,194},{1... | collective-permute-start | bytes 49160 | tf_op jit(solution)/shard_map/ppermute | solution.py:18
  5.9 1.3 collective-permute-start.1
  7.2 0.1 and_and_fusion.8
  7.4 0.1 and_and_fusion.6
  7.5 0.1 and_and_fusion.2
  7.6 3.3 %collective-permute-done.1 = f32[32,4,1,32]{3,2,0,1:T(1,128)S(1)} collective-permute-done((f32[32,4,1,32]{3,2,0,1:T(1,128)S(1)}, f32[32,4,1,32]{3,2,0,1:T(1,128)S(1)}, u32[]{:S(2)}, u32[]{:S(2)}) %collective-permute-start.1) | collective-permute-done | bytes 16416 | tf_op jit(solution)/shard_map/ppermute | solution.py:20
  10.9 0.2 pad_maximum_fusion.6
  11.2 5.1 %collective-permute-start.2 = (f32[32,1,10,32]{3,2,0,1:T(8,128)S(1)}, f32[32,1,10,32]{3,2,0,1:T(8,128)S(1)}, u32[]{:S(2)}, u32[]{:S(2)}) collective-permute-start(f32[32,1,10,32]{3,2,0,1:T(8,128)S(1)} %get-tuple-element.11), channel_id=1, source_target_pairs={{0,24},{24,48},{48,72},{72,96},{96,120},{120,144},{144,168},{1,25}... | collective-permute-start | bytes 122888 | tf_op jit(solution)/shard_map/ppermute | solution.py:18
  16.4 7.0 %collective-permute-start.3 = (f32[32,1,10,32]{3,2,0,1:T(8,128)S(1)}, f32[32,1,10,32]{3,2,0,1:T(8,128)S(1)}, u32[]{:S(2)}, u32[]{:S(2)}) collective-permute-start(f32[32,1,10,32]{3,2,0,1:T(8,128)S(1)} %get-tuple-element.12), channel_id=1, source_target_pairs={{24,0},{48,24},{72,48},{96,72},{120,96},{144,120},{168,144},{25,1}... | collective-permute-start | bytes 122888 | tf_op jit(solution)/shard_map/ppermute | solution.py:20
  23.5 1.0 collective-permute-done.3
  24.5 0.3 maximum_multiply_fusion
  24.9 0.1 slice_add_fusion
  25.0 0.3 fusion.9
  25.3 0.2 slice_add_fusion.2
  25.5 0.9 fusion.80
  26.4 0.2 stack.91
  26.6 0.2 stack.92
  26.8 0.8 copy.22
  27.5 5.8 %all-to-all-start = ((bf16[2,32,4,256]{3,2,0,1:T(4,128)(2,1)}), bf16[2,32,4,256]{3,2,0,1:T(4,128)(2,1)S(1)}, u32[]{:S(2)}, u32[]{:S(2)}) async-start(bf16[2,32,4,256]{3,2,0,1:T(4,128)(2,1)} %copy.22), calls=%async_computation | async-start | bytes 262144 | tf_op jit(solution)/shard_map/all_to_all | solution.py:58
  33.4 0.1 and_and_fusion
  33.4 8.5 %all-to-all-done = bf16[2,32,4,256]{3,2,0,1:T(4,128)(2,1)S(1)} async-done(((bf16[2,32,4,256]{3,2,0,1:T(4,128)(2,1)}), bf16[2,32,4,256]{3,2,0,1:T(4,128)(2,1)S(1)}, u32[]{:S(2)}, u32[]{:S(2)}) %all-to-all-start) | async-done | bytes 131104 | tf_op jit(solution)/shard_map/all_to_all | solution.py:58
  41.9 0.1 copy.23
  42.0 0.1 copy.24
  42.1 0.1 squeeze_reshape_transpose_reshape.5
  42.2 0.1 squeeze_reshape_transpose_reshape.6
  42.2 1.0 fusion.19
  43.2 0.9 fusion.25
  44.1 0.9 fusion.31
  45.1 1.0 fusion.37
  46.1 0.9 fusion.43
  46.9 1.0 fusion.47
  47.9 0.9 fusion.53
  48.8 1.0 fusion.59
  49.8 0.9 fusion.65
  50.7 1.0 fusion.21
  51.7 1.0 fusion.27
  52.7 1.0 fusion.33
  53.6 1.0 fusion.39
  54.6 0.8 fusion.70
  55.4 1.0 fusion.49
  56.4 1.0 fusion.55
  57.4 1.0 fusion.61
  58.3 0.9 fusion.67
  59.3 0.9 fusion.23
  60.2 0.9 fusion.29
  61.2 1.0 fusion.35
  62.1 0.9 fusion.41
  63.1 0.9 fusion.45
  63.9 1.0 fusion.51
  64.9 1.0 fusion.57
  65.9 0.9 fusion.63
  66.8 0.9 fusion.69
  67.8 8.6 %reshape.84 = bf16[54,32768]{1,0:T(8,128)(2,1)} reshape(bf16[27,2,32768]{2,1,0:T(2,128)(2,1)} %fusion.69) | data formatting | bytes 7077888 | tf_op jit(solution)/shard_map/reshape | solution.py:71
  76.3 3.3 %fusion = f32[64,32768]{1,0:T(8,128)S(1)} fusion(bf16[54,32768]{1,0:T(8,128)(2,1)} %reshape.84, bf16[54,64]{1,0:T(8,128)(2,1)S(1)} %copy-done.2, f32[64]{0:T(128)S(1)} %copy-done.3), kind=kOutput, calls=%fused_computation.2 | convolution fusion | flops 228589568 | bytes 11934720 | tf_op jit(solution)/shard_map/kc,kh->hc/dot_general | solution.py:77
  79.7 4.1 %exponential_reduce_fusion = (f32[32768]{0:T(1024)S(1)}, f32[64,32768]{1,0:T(8,128)S(1)}) fusion(f32[64]{0:T(128)S(1)} %copy-done.4, bf16[64,64]{1,0:T(8,128)(2,1)S(1)} %copy-done, f32[64,32768]{1,0:T(8,128)S(1)} %fusion), kind=kOutput, calls=%fused_computation.12 | convolution fusion | flops 283082752 | bytes 16916736 | tf_op jit(solution)/shard_map/hb,hc->bc/dot_general | solution.py:82
  83.8 3.7 %fusion.6 = f32[64,64]{1,0:T(8,128)S(1)} fusion(f32[64,32768]{1,0:T(8,128)S(1)} %fusion, f32[64,32768]{1,0:T(8,128)S(1)} %get-tuple-element.18, f32[32768]{0:T(1024)S(1)} %get-tuple-element.17, s32[32768]{0:T(1024)S(1)} %bitcast.137), kind=kOutput, calls=%fused_computation.15 | convolution fusion | flops 291504128 | bytes 17055744 | tf_op jit(solution)/shard_map/hc,bc->hb/dot_general | solution.py:92
  87.4 7.4 %fusion.84 = (f32[64]{0:T(128)S(1)}, bf16[64,32768]{1,0:T(8,128)(2,1)}) fusion(f32[64,32768]{1,0:T(8,128)S(1)} %fusion, bf16[64,64]{1,0:T(8,128)(2,1)S(1)} %copy-done, s32[32768]{0:T(1024)S(1)} %bitcast.138, f32[32768]{0:T(1024)S(1)} %get-tuple-element.17, f32[64,32768]{1,0:T(8,128)S(1)} %get-tuple-element.18), kind=kOutput, calls=%fused_computation.157 | convolution fusion | flops 301989824 | bytes 21242112 | tf_op jit(solution)/shard_map/hb,bc->hc/dot_general | solution.py:96
  94.9 4.5 %fusion.81 = (f32[64]{0:T(128)S(1)}, f32[32768]{0:T(1024)S(1)}) fusion(s32[32768]{0:T(1024)S(1)} %bitcast.139, f32[32768]{0:T(1024)S(1)} %get-tuple-element.17, f32[64,32768]{1,0:T(8,128)S(1)} %get-tuple-element.18), kind=kLoop, calls=%fused_computation.154 | loop fusion | flops 16744384 | bytes 8782080 | tf_op jit(solution)/shard_map/reduce_sum | solution.py:95
  99.4 0.7 sub.135
  100.1 4.5 %fusion.4 = f32[54,64]{1,0:T(8,128)S(1)} fusion(bf16[54,32768]{1,0:T(8,128)(2,1)} %reshape.84, bf16[64,32768]{1,0:T(8,128)(2,1)} %get-tuple-element.20), kind=kOutput, calls=%fused_computation.13 | convolution fusion | flops 226492416 | bytes 7747072 | tf_op jit(solution)/shard_map/kc,hc->kh/dot_general | solution.py:103
  104.6 116.0 %all-reduce.3 = (f32[54,64]{1,0:T(8,128)}, f32[64]{0:T(128)}, f32[64,64]{1,0:T(8,128)}, f32[64]{0:T(128)}) all-reduce(f32[54,64]{1,0:T(8,128)S(1)} %fusion.4, f32[64]{0:T(128)S(1)} %get-tuple-element.19, f32[64,64]{1,0:T(8,128)S(1)} %fusion.6, f32[64]{0:T(128)S(1)} %get-tuple-element.5), channel_id=1, replica_groups=mesh['sec'=4,'sp'=8,'dp'=24] {'sec','sp','dp'}, use_global_device_ids=true, to_apply=%region_2.3 | all-reduce | flops 7680 | bytes 61440 | tf_op jit(solution)/shard_map/psum | solution.py:135
  (20 shorter events, 0.3 us)
Async XLA Ops:
  0.6 79.0 %copy-start = (bf16[64,64]{1,0:T(8,128)(2,1)S(1)}, bf16[64,64]{1,0:T(8,128)(2,1)}, u32[]{:S(2)}) copy-start(bf16[64,64]{1,0:T(8,128)(2,1)} %param.10) | copy-start | bytes 24580
  0.6 22.8 %copy-start.1 = (s32[1,1,32,1024]{3,2,1,0:T(8,128)S(1)}, s32[1,1,32,1024]{3,2,1,0:T(8,128)}, u32[]{:S(2)}) copy-start(s32[1,1,32,1024]{3,2,1,0:T(8,128)} %param.7) | copy-start | bytes 393220
  1.9 5.7 %collective-permute-start = (f32[32,4,1,32]{3,2,0,1:T(1,128)S(1)}, f32[32,4,1,32]{3,2,0,1:T(1,128)S(1)}, u32[]{:S(2)}, u32[]{:S(2)}) collective-permute-start(f32[32,4,1,32]{3,2,0,1:T(1,128)S(1)} %get-tuple-element.15), channel_id=1, source_target_pairs={{0,192},{192,384},{384,576},{1,193},{193,385},{385,577},{2,194},{1... | collective-permute-start | bytes 49160 | tf_op jit(solution)/shard_map/ppermute | solution.py:18
  5.9 5.0 %collective-permute-start.1 = (f32[32,4,1,32]{3,2,0,1:T(1,128)S(1)}, f32[32,4,1,32]{3,2,0,1:T(1,128)S(1)}, u32[]{:S(2)}, u32[]{:S(2)}) collective-permute-start(f32[32,4,1,32]{3,2,0,1:T(1,128)S(1)} %get-tuple-element.16), channel_id=1, source_target_pairs={{192,0},{384,192},{576,384},{193,1},{385,193},{577,385},{194,2},{3... | collective-permute-start | bytes 49160 | tf_op jit(solution)/shard_map/ppermute | solution.py:20
  11.2 12.3 %collective-permute-start.2 = (f32[32,1,10,32]{3,2,0,1:T(8,128)S(1)}, f32[32,1,10,32]{3,2,0,1:T(8,128)S(1)}, u32[]{:S(2)}, u32[]{:S(2)}) collective-permute-start(f32[32,1,10,32]{3,2,0,1:T(8,128)S(1)} %get-tuple-element.11), channel_id=1, source_target_pairs={{0,24},{24,48},{48,72},{72,96},{96,120},{120,144},{144,168},{1,25}... | collective-permute-start | bytes 122888 | tf_op jit(solution)/shard_map/ppermute | solution.py:18
  16.4 8.2 %collective-permute-start.3 = (f32[32,1,10,32]{3,2,0,1:T(8,128)S(1)}, f32[32,1,10,32]{3,2,0,1:T(8,128)S(1)}, u32[]{:S(2)}, u32[]{:S(2)}) collective-permute-start(f32[32,1,10,32]{3,2,0,1:T(8,128)S(1)} %get-tuple-element.12), channel_id=1, source_target_pairs={{24,0},{48,24},{72,48},{96,72},{120,96},{144,120},{168,144},{25,1}... | collective-permute-start | bytes 122888 | tf_op jit(solution)/shard_map/ppermute | solution.py:20
  27.5 14.4 %all-to-all-start = ((bf16[2,32,4,256]{3,2,0,1:T(4,128)(2,1)}), bf16[2,32,4,256]{3,2,0,1:T(4,128)(2,1)S(1)}, u32[]{:S(2)}, u32[]{:S(2)}) async-start(bf16[2,32,4,256]{3,2,0,1:T(4,128)(2,1)} %copy.22), calls=%async_computation | async-start | bytes 262144 | tf_op jit(solution)/shard_map/all_to_all | solution.py:58
  67.8 8.6 %copy-start.2 = (bf16[54,64]{1,0:T(8,128)(2,1)S(1)}, bf16[54,64]{1,0:T(8,128)(2,1)}, u32[]{:S(2)}) copy-start(bf16[54,64]{1,0:T(8,128)(2,1)} %param.8) | copy-start | bytes 20740
  67.8 8.6 %copy-start.3 = (f32[64]{0:T(128)S(1)}, f32[64]{0:T(128)}, u32[]{:S(2)}) copy-start(f32[64]{0:T(128)} %param.9) | copy-start | bytes 772
  76.3 3.4 %copy-start.4 = (f32[64]{0:T(128)S(1)}, f32[64]{0:T(128)}, u32[]{:S(2)}) copy-start(f32[64]{0:T(128)} %param.11) | copy-start | bytes 772
where the time goes:
time: 221 us
  blocking collectives  116 us (52%)
  other arithmetic  32.6 us (15%)
  starting transfers between devices  23.3 us (11%)
  matrix products  23 us (10%)
  waiting for transfers between devices  12.8 us (6%)
  local copies, waits for them, and re-layouts  12 us (5%)
    psum x1, blocking collectives, shards(): lax.psum((conv_wsum, conv_bsum, out_wsum, out_bsum), ('sec', 'sp', 'dp'))  116 us
    unnamed x26, other arithmetic  24.5 us
    ppermute x2, starting transfers between devices, extended(): lax.ppermute(tail, axis, [(i, (i + 1) % count) for i in range(ends)])  9.14 us
    reshape x1, local copies, waits for them, and re-layouts, make_columns(): return stacked.reshape(2 * stacked.shape[0], stacked.shape[2])  8.56 us
    all_to_all x1, waiting for transfers between devices, relay_features(): lax.all_to_all(block, ('sec', 'sp'), split_axis=1, concat_axis=2, tiled=T...  8.47 us
    ppermute x2, starting transfers between devices, extended(): lax.ppermute(head, axis, [((i + 1) % count, i) for i in range(ends)])  8.32 us
    dot_general x1, matrix products, patch_step(): jnp.einsum('hb,bc->hc', out_weight, residual_low, preferred_element_type=...  7.44 us
    all_to_all x1, starting transfers between devices, relay_features(): lax.all_to_all(block, ('sec', 'sp'), split_axis=1, concat_axis=2, tiled=T...  5.82 us
  transfers between devices with their start and end apart: 5, of which 3 were waited for; matrix products, arithmetic and copies ran while one was open for 0% of the time, Pallas kernels for 0%

commit v1 on v0

v1 whole, which is shorter than its diff:
```python
import functools
import jax
import jax.numpy as jnp
from jax import lax
from jax.experimental import pallas as pl
from jax.experimental.pallas import tpu as pltpu
from jax.sharding import PartitionSpec as P

PX, PY, PZ = 32, 32, 32
PLANE = PY * PZ
HID = 64
BINS = 64
FEATS = 54
XB = 8
NB = PX // XB
GROUP = 24
KC = 9 * GROUP
KP = KC + 8
KO = HID + 16
TILE = 256
F32, BF16 = jnp.float32, jnp.bfloat16
LEAD = 3
CH = 2
NT = (((1,), (1,)), ((), ()))
TN = (((0,), (0,)), ((), ()))


def iota(shape, axis):
    return lax.broadcasted_iota(jnp.int32, shape, axis)


def split3(value):
    high = value.astype(BF16)
    rest = value - high.astype(F32)
    mid = rest.astype(BF16)
    low = (rest - mid.astype(F32)).astype(BF16)
    return high.astype(F32), mid.astype(F32), low.astype(F32)


def column(row):
    n = row.shape[1]
    eye = iota((n, n), 0) == iota((n, n), 1)
    return jnp.sum(jnp.where(eye, row, 0.0), axis=1, keepdims=True)


def conv_rows(p_minus_x, shape, k_axis, c_axis):
    col = iota(shape, c_axis)
    k = iota(shape, k_axis)
    t = col // GROUP
    u = col - t * GROUP
    c = jnp.where(u >= 10, 1, 0)
    dx = u - 10 * c - p_minus_x
    return (col < KC) & (u < 20) & (dx >= 0) & (dx < 3) & (k == 18 * dx + 2 * t + c)


def prepare(cw_ref, cb_ref, ow_ref, ob_ref, wide_ref, owt_ref, owb_ref):
    cb = column(cb_ref[...].reshape(1, HID)) * 0.5
    ch, cm, cl = split3(cb)
    col = iota((HID, KP), 1)
    bias = jnp.where(col == KC, ch, jnp.where(col == KC + 1, cm, jnp.where(col == KC + 2, cl, 0.0)))
    cw = cw_ref[...]
    for x in range(XB):
        pick = jnp.where(conv_rows(x, (FEATS, KP), 0, 1), 0.5, 0.0).astype(BF16)
        row = lax.dot_general(cw, pick, TN, preferred_element_type=F32) + bias
        wide_ref[x * HID:(x + 1) * HID, :] = row.astype(BF16)
    ob = column(ob_ref[...].reshape(1, BINS))
    oh, om, ol = split3(ob)
    ow = ow_ref[...]
    eye = (iota((HID, KO), 0) == iota((HID, KO), 1)).astype(F32).astype(BF16)
    owt = lax.dot_general(ow, eye, TN, preferred_element_type=F32)
    col = iota((BINS, KO), 1)
    owt = owt + jnp.where(col == HID, oh, jnp.where(col == HID + 1, om, jnp.where(col == HID + 2, ol, 0.0)))
    owt_ref[...] = owt.astype(BF16)
    owb_ref[...] = (ow.astype(F32) * 0.5).astype(BF16)


def box(padded_ref, square, z_lo, z_hi, y_lo, y_hi):
    a, b, c = padded_ref[7:39, :], padded_ref[8:40, :], padded_ref[9:41, :]
    if square:
        s = a * a + b * b + c * c
    else:
        s = a + b + c
    s = s + jnp.where(z_lo, 0.0, pltpu.roll(s, 1, 1)) + jnp.where(z_hi, 0.0, pltpu.roll(s, PLANE - 1, 1))
    s = s + jnp.where(y_lo, 0.0, pltpu.roll(s, PZ, 1)) + jnp.where(y_hi, 0.0, pltpu.roll(s, PLANE - PZ, 1))
    return s / 27.0


def edges(shape):
    pos = iota(shape, 1)
    z = pos & (PZ - 1)
    return z == 0, z == PZ - 1, pos < PZ, pos >= PLANE - PZ


def filter_patch(patch_ref, pad_ref, f0_ref, f1_ref):
    zero = jnp.zeros((8, PLANE), F32)
    for ref in (pad_ref, f0_ref, f1_ref):
        ref[0:8, :] = zero
        ref[40:48, :] = zero
    for i in range(8):
        pad_ref[8 + 4 * i:12 + 4 * i, :] = patch_ref[i]
    z_lo, z_hi, y_lo, y_hi = edges((PX, PLANE))
    filt = box(pad_ref, False, z_lo, z_hi, y_lo, y_hi)
    f0_ref[8:40, :] = filt
    f1_ref[8:40, :] = box(pad_ref, True, z_lo, z_hi, y_lo, y_hi) - filt * filt


def stencil(f0_ref, f1_ref, join_ref, g_ref):
    z_lo, z_hi, y_lo, y_hi = edges((GROUP, PLANE))
    join_ref[20:24, :] = jnp.zeros((4, PLANE), F32)
    for b in range(NB):
        join_ref[0:10, :] = f0_ref[8 * b + 7:8 * b + 17, :]
        join_ref[10:20, :] = f1_ref[8 * b + 7:8 * b + 17, :]
        mid = join_ref[...]
        lo = jnp.where(z_lo, 0.0, pltpu.roll(mid, 1, 1))
        hi = jnp.where(z_hi, 0.0, pltpu.roll(mid, PLANE - 1, 1))
        parts = []
        for step_y in (-1, 0, 1):
            for v in (lo, mid, hi):
                if step_y == -1:
                    v = jnp.where(y_lo, 0.0, pltpu.roll(v, PZ, 1))
                elif step_y == 1:
                    v = jnp.where(y_hi, 0.0, pltpu.roll(v, PLANE - PZ, 1))
                parts.append(v)
        parts.append(jnp.ones((8, PLANE), F32))
        g_ref[b] = jnp.concatenate(parts, axis=0).astype(BF16)


def fold(v):
    return v[:, :128] + v[:, 128:]


def train(labels_ref, wide_ref, owt_ref, owb_ref, g_ref, act_ref, d_ref, low_ref, grad_ref, z_ref, pick_ref, dconv_ref, dout_ref, hsum_ref, rsum_ref, scale):
    dconv_ref[...] = jnp.zeros_like(dconv_ref)
    dout_ref[...] = jnp.zeros_like(dout_ref)
    hsum_ref[...] = jnp.zeros_like(hsum_ref)
    rsum_ref[...] = jnp.zeros_like(rsum_ref)
    low_ref[...] = jnp.zeros_like(low_ref)
    grad_ref[...] = jnp.zeros_like(grad_ref)
    act_ref[...] = jnp.zeros_like(act_ref)
    bins = iota((BINS, TILE), 0)
    ones = jnp.ones((16, TILE), BF16)
    width = CH * TILE
    per = PLANE // width
    steps = NB * per

    def place(step, c):
        b = step // per
        return b, pl.ds(pl.multiple_of((step % per) * width + c * TILE, TILE), TILE)

    def whole(step):
        b = step // per
        return b, pl.ds(pl.multiple_of((step % per) * width, width), width)

    def ahead(step, slot, c):
        b, cols = place(step, c)
        u_all = jnp.dot(wide_ref[...], g_ref[b, :, cols], preferred_element_type=F32)
        for x in range(XB):
            u = u_all[x * HID:(x + 1) * HID]
            t = jnp.tanh(u)
            w = 1.0 + t
            a = u * w
            act_ref[slot, x, :, c * TILE:(c + 1) * TILE] = a.astype(BF16)
            d_ref[slot, x, :, c * TILE:(c + 1) * TILE] = (w + a) - a * t

    def behind_out(step, act_slot, slot):
        dout_ref[...] += lax.dot_general(
            jnp.concatenate([act_ref[act_slot, x] for x in range(XB)], axis=1),
            jnp.concatenate([low_ref[slot, x] for x in range(XB)], axis=1), NT, preferred_element_type=F32)

    def behind_conv(step, slot):
        b, cols = whole(step)
        dconv_ref[...] += lax.dot_general(grad_ref[slot], g_ref[b, :, cols], NT, preferred_element_type=F32)

    for c in range(CH):
        ahead(0, 0, c)

    def body(step, carry):
        slot = lax.rem(step, 2)
        slot3 = lax.rem(step, 3)
        next3 = lax.rem(step + 1, 3)
        last3 = lax.rem(step + 2, 3)
        last = jnp.maximum(step - 1, 0)

        def project(c, x):
            return jnp.dot(owt_ref[...], jnp.concatenate([act_ref[slot3, x, :, c * TILE:(c + 1) * TILE], ones], axis=0), preferred_element_type=F32)

        tiles = [(c, x) for c in range(CH) for x in range(XB)]
        count = len(tiles)
        logits_of = {i: project(*tiles[i]) for i in range(LEAD)}
        backs = {}
        hsum = rsum = None
        for i in range(count + 1):
            if i < count:
                c, x = tiles[i]
                span = slice(c * TILE, (c + 1) * TILE)
                b, cols = place(step, c)
                logits = logits_of.pop(i)
                if i + LEAD < count:
                    logits_of[i + LEAD] = project(*tiles[i + LEAD])
                if i % XB == 0:
                    ahead_at(ahead, step, next3, c, steps)
                e = jnp.exp(logits)
                row = XB * b + x
                hit = bins == labels_ref[pl.ds(row, 1), cols]
                total = jnp.sum(e, axis=0, keepdims=True)
                z_ref[pl.ds(row, 1), cols] = total
                pick_ref[pl.ds(row, 1), cols] = jnp.sum(jnp.where(hit, logits, 0.0), axis=0, keepdims=True)
                r = e * (scale / total) - jnp.where(hit, scale, 0.0)
                low = r.astype(BF16)
                low_ref[slot, x, :, span] = low
                rsum = fold(r) if rsum is None else rsum + fold(r)
                backs[i] = jnp.dot(owb_ref[...], low, preferred_element_type=F32)
                if i == count // 4:
                    behind_out(last, last3, 1 - slot)
                if i == count // 2:
                    behind_conv(last, 1 - slot)
            if i >= 1:
                c, x = tiles[i - 1]
                span = slice(c * TILE, (c + 1) * TILE)
                grad = backs.pop(i - 1) * d_ref[slot3, x, :, span]
                grad_ref[slot, x * HID:(x + 1) * HID, span] = grad.astype(BF16)
                hsum = fold(grad) if hsum is None else hsum + fold(grad)
        hsum_ref[...] += hsum
        rsum_ref[...] += rsum
        return carry

    lax.fori_loop(0, steps, body, 0)
    behind_out(steps - 1, (steps - 1) % 3, (steps - 1) % 2)
    behind_conv(steps - 1, (steps - 1) % 2)


def ahead_at(ahead, step, slot, c, steps):
    ahead(jnp.minimum(step + 1, steps - 1), slot, c)


def finish(z_ref, pick_ref, dconv_ref, dout_ref, hsum_ref, rsum_ref, loss_ref, part_ref):
    loss_ref[...] = jnp.log(z_ref[...]) - pick_ref[...]
    total = dconv_ref[0:HID, :]
    for x in range(1, XB):
        total = total + pltpu.roll(dconv_ref[x * HID:(x + 1) * HID, :], KP - x, 1)
    col = iota((HID, KP), 1)
    hcol = jnp.sum(hsum_ref[...], axis=1, keepdims=True)
    rcol = jnp.sum(rsum_ref[...], axis=1, keepdims=True)
    total = jnp.where(col == KC, hcol, jnp.where(col == KC + 1, rcol, total))
    k, c = iota((HID, KP), 0), iota((HID, KP), 1)
    pick = conv_rows(0, (HID, KP), 0, 1) | ((k == FEATS) & (c == KC)) | ((k == FEATS + 1) & (c == KC + 1))
    rows = lax.dot_general(jnp.where(pick, 1.0, 0.0), total, NT, precision=lax.Precision.HIGHEST, preferred_element_type=F32)
    part_ref[:, 0:HID] = rows
    part_ref[:, HID:2 * HID] = dout_ref[...]


def compute_scratch():
    return [
        pltpu.VMEM((48, PLANE), F32), pltpu.VMEM((48, PLANE), F32), pltpu.VMEM((48, PLANE), F32),
        pltpu.VMEM((GROUP, PLANE), F32),
        pltpu.VMEM((NB, KP, PLANE), BF16),
        pltpu.VMEM((XB * HID, KP), BF16), pltpu.VMEM((BINS, KO), BF16), pltpu.VMEM((HID, BINS), BF16),
        pltpu.VMEM((3, XB, HID, CH * TILE), BF16), pltpu.VMEM((3, XB, HID, CH * TILE), F32),
        pltpu.VMEM((2, XB, BINS, CH * TILE), BF16), pltpu.VMEM((2, XB * HID, CH * TILE), BF16),
        pltpu.VMEM((PX, PLANE), F32), pltpu.VMEM((PX, PLANE), F32),
        pltpu.VMEM((XB * HID, KP), F32), pltpu.VMEM((HID, BINS), F32),
        pltpu.VMEM((HID, 128), F32), pltpu.VMEM((BINS, 128), F32),
    ]


def compute_kernel(scale, stages, patch_ref, labels_ref, cw_ref, cb_ref, ow_ref, ob_ref, loss_ref, part_ref,
                   pad, f0, f1, join, g, wide, owt, owb, act, d, low, grad, z, pick, dconv, dout, hsum, rsum):
    if "p" in stages:
        prepare(cw_ref, cb_ref, ow_ref, ob_ref, wide, owt, owb)
    if "f" in stages:
        filter_patch(patch_ref, pad, f0, f1)
    if "s" in stages:
        stencil(f0, f1, join, g)
    if "t" in stages:
        train(labels_ref, wide, owt, owb, g, act, d, low, grad, z, pick, dconv, dout, hsum, rsum, scale)
    if "e" in stages:
        finish(z, pick, dconv, dout, hsum, rsum, loss_ref, part_ref)


def compute(patch, labels, cw, cb, ow, ob, scale, stages="pfste"):
    vm = pl.BlockSpec(memory_space=pltpu.VMEM)
    return pl.pallas_call(
        functools.partial(compute_kernel, scale, stages),
        out_shape=(jax.ShapeDtypeStruct((PX, PLANE), F32), jax.ShapeDtypeStruct((HID, 128), F32)),
        in_specs=[vm] * 6,
        out_specs=(vm, vm),
        scratch_shapes=compute_scratch(),
        compiler_params=pltpu.CompilerParams(vmem_limit_bytes=48 * 2**20),
        name="train_patch",
    )(patch, labels, cw, cb, ow, ob)


SEC, SP, DP = 4, 8, 24
TEAM = SEC * SP
PIECE = HID // TEAM


def team_rank():
    return lax.axis_index("sec") * SP + lax.axis_index("sp")


def team_device(rank):
    return {"sec": rank // SP, "sp": rank % SP}


def greet(team, replicas):
    barrier = pltpu.get_barrier_semaphore()
    if team:
        me = team_rank()

        def hail(i, carry):
            pl.semaphore_signal(barrier, inc=1, device_id=team_device(lax.rem(me + i, TEAM)), device_id_type=pl.DeviceIdType.MESH)
            return carry

        lax.fori_loop(1, TEAM, hail, 0)
    if replicas:
        mine = lax.axis_index("dp")

        def call(i, carry):
            pl.semaphore_signal(barrier, inc=1, device_id={"dp": lax.rem(mine + i, DP)}, device_id_type=pl.DeviceIdType.MESH)
            return carry

        lax.fori_loop(1, DP, call, 0)
    pl.semaphore_wait(barrier, (TEAM - 1) * team + (DP - 1) * replicas)


def relay_kernel(frac_ref, patch_ref, own_sem, send_sems, recv_sems):
    greet(1, 0)
    me = team_rank()
    sec, sp = lax.axis_index("sec"), lax.axis_index("sp")
    spot = patch_ref.at[sp, :, pl.ds(pl.multiple_of(sec * TILE, TILE), TILE)]

    def parcel(rank, sender):
        return pltpu.make_async_remote_copy(
            src_ref=frac_ref.at[rank], dst_ref=spot, send_sem=send_sems.at[rank], recv_sem=recv_sems.at[sender],
            device_id=team_device(rank), device_id_type=pl.DeviceIdType.MESH)

    def send(i, carry):
        parcel(lax.rem(me + i, TEAM), me).start()
        return carry

    lax.fori_loop(1, TEAM, send, 0)
    own = pltpu.make_async_copy(frac_ref.at[me], spot, own_sem)
    own.start()

    def settle(i, carry):
        other = lax.rem(me + i, TEAM)
        parcel(other, other).wait()
        return carry

    lax.fori_loop(1, TEAM, settle, 0)
    own.wait()


def relay(frac):
    return pl.pallas_call(
        relay_kernel,
        out_shape=jax.ShapeDtypeStruct((SP, 4, PLANE), F32),
        in_specs=[pl.BlockSpec(memory_space=pl.ANY)],
        out_specs=pl.BlockSpec(memory_space=pltpu.VMEM),
        scratch_shapes=[pltpu.SemaphoreType.DMA, pltpu.SemaphoreType.DMA((TEAM,)), pltpu.SemaphoreType.DMA((TEAM,))],
        compiler_params=pltpu.CompilerParams(collective_id=0, has_side_effects=True),
        name="relay_patches",
    )(frac)


def swap(ref, slots, sends, recvs, count, me, device, source):
    def parcel(rank, sender):
        return pltpu.make_async_remote_copy(
            src_ref=source(rank), dst_ref=slots.at[sender], send_sem=sends.at[rank], recv_sem=recvs.at[sender],
            device_id=device(rank), device_id_type=pl.DeviceIdType.MESH)

    def send(i, carry):
        parcel(lax.rem(me + i, count), me).start()
        return carry

    lax.fori_loop(1, count, send, 0)

    def settle(i, carry):
        other = lax.rem(me + i, count)
        parcel(other, other).wait()
        return carry

    lax.fori_loop(1, count, settle, 0)


def reduce_kernel(part_ref, conv_ref, cbias_ref, out_ref, obias_ref, split, first, piece, second, total, result,
                  s1, r1, s2, r2, s3, r3):
    greet(1, 1)
    me, mine = team_rank(), lax.axis_index("dp")
    for j in range(TEAM):
        split[j] = part_ref[PIECE * j:PIECE * (j + 1), :]
    first[me] = split[me]
    swap(None, first, s1, r1, TEAM, me, team_device, lambda rank: split.at[rank])
    piece[...] = jnp.sum(first[...], axis=0)
    second[mine] = piece[...]
    swap(None, second, s2, r2, DP, mine, lambda rank: {"dp": rank}, lambda rank: piece)
    total[...] = jnp.sum(second[...], axis=0)
    result[me] = total[...]
    swap(None, result, s3, r3, TEAM, me, team_device, lambda rank: total)
    for j in range(TEAM):
        lo = PIECE * j
        both = result[j]
        out_ref[lo:lo + PIECE, :] = both[:, HID:]
        if lo < FEATS:
            conv_ref[lo:lo + PIECE, :] = both[:, :HID]
        elif lo == FEATS:
            cbias_ref[...] = both[0:1, :HID]
            obias_ref[...] = both[1:2, :HID]


def reduce_grads(part):
    vm = pl.BlockSpec(memory_space=pltpu.VMEM)
    return pl.pallas_call(
        reduce_kernel,
        out_shape=(jax.ShapeDtypeStruct((FEATS, HID), F32), jax.ShapeDtypeStruct((1, HID), F32),
                   jax.ShapeDtypeStruct((HID, BINS), F32), jax.ShapeDtypeStruct((1, BINS), F32)),
        in_specs=[vm],
        out_specs=(vm, vm, vm, vm),
        scratch_shapes=[
            pltpu.VMEM((TEAM, PIECE, 128), F32), pltpu.VMEM((TEAM, PIECE, 128), F32), pltpu.VMEM((PIECE, 128), F32),
            pltpu.VMEM((DP, PIECE, 128), F32), pltpu.VMEM((PIECE, 128), F32), pltpu.VMEM((TEAM, PIECE, 128), F32),
            pltpu.SemaphoreType.DMA((TEAM,)), pltpu.SemaphoreType.DMA((TEAM,)),
            pltpu.SemaphoreType.DMA((DP,)), pltpu.SemaphoreType.DMA((DP,)),
            pltpu.SemaphoreType.DMA((TEAM,)), pltpu.SemaphoreType.DMA((TEAM,)),
        ],
        compiler_params=pltpu.CompilerParams(collective_id=1, has_side_effects=True),
        name="reduce_grads",
    )(part)


def shards(fraction, labels, conv_weight, conv_bias, out_weight, out_bias):
    patch = relay(fraction.reshape(fraction.shape[1:]))
    loss, part = compute(patch, labels.reshape(PX, PLANE), conv_weight, conv_bias, out_weight, out_bias, 1.0 / 25165824)
    conv, cbias, out, obias = reduce_grads(part)
    return loss.reshape(labels.shape), conv, cbias.reshape(HID), out, obias.reshape(BINS)


def solution(mesh):
    placed = (P("dp", None, "sp", "sec"), P("dp", ("sec", "sp"), None, None), P(), P(), P(), P())
    return jax.shard_map(
        shards,
        mesh=mesh,
        in_specs=placed,
        out_specs=(P("dp", ("sec", "sp"), None, None), P(), P(), P(), P()),
        check_vma=False,
    )
```

time: 221 us -> 75.9 us (0.34)
  blocking collectives: 116 us -> 0 us
  Pallas kernels: 0 us -> 70.3 us
  other arithmetic: 32.6 us -> 0 us
  starting transfers between devices: 23.3 us -> 0 us
  matrix products: 23 us -> 0 us
  waiting for transfers between devices: 12.8 us -> 0 us
  local copies, waits for them, and re-layouts: 12 us -> 4.54 us
    psum x1 -> x0, blocking collectives: 116 us -> none  [shards(): lax.psum((conv_wsum, conv_bsum, out_wsum, out_bsum), ('sec', 'sp', 'dp'))]
    pallas_call x0 -> x3, Pallas kernels: none -> 70.3 us  [the longest x1 33.1 us: reduce_grads(): pl.pallas_call(reduce_kernel, out_shape=(jax.ShapeDtypeStruct((FEATS, HID...]
    unnamed x26 -> x0, other arithmetic: 24.5 us -> none
    dot_general x5 -> x0, matrix products: 23 us -> none  [the longest x1 7.44 us: patch_step(): jnp.einsum('hb,bc->hc', out_weight, residual_low, preferred_element_type=...]
    ppermute x4 -> x0, starting transfers between devices: 17.5 us -> none  [the longest x2 9.14 us: extended(): lax.ppermute(tail, axis, [(i, (i + 1) % count) for i in range(ends)])]
    reshape x1 -> x0, local copies, waits for them, and re-layouts: 8.56 us -> none  [make_columns(): return stacked.reshape(2 * stacked.shape[0], stacked.shape[2])]
    all_to_all x1 -> x0, waiting for transfers between devices: 8.47 us -> none  [relay_features(): lax.all_to_all(block, ('sec', 'sp'), split_axis=1, concat_axis=2, tiled=T...]
    all_to_all x1 -> x0, starting transfers between devices: 5.82 us -> none  [relay_features(): lax.all_to_all(block, ('sec', 'sp'), split_axis=1, concat_axis=2, tiled=T...]
  transfers between devices with their start and end apart: 5 -> 0, of which waited for: 3 -> 0; matrix products, arithmetic and copies ran while one was open for 0% -> 0% of each run, Pallas kernels for 0% -> 0%
where the time goes in v1:
time: 75.9 us; the launch traced here: 75.6 us
  Pallas kernels  70.3 us (93%)
  local copies, waits for them, and re-layouts  4.54 us (6%)
  between operations  0.76 us (1%)
    pallas_call x1, Pallas kernels, reduce_grads(): pl.pallas_call(reduce_kernel, out_shape=(jax.ShapeDtypeStruct((FEATS, HID...  33.1 us
    pallas_call x1, Pallas kernels, relay(): pl.pallas_call(relay_kernel, out_shape=jax.ShapeDtypeStruct((SP, 4, PLANE...  20.9 us
    pallas_call x1, Pallas kernels, compute(): pl.pallas_call(functools.partial(compute_kernel, scale, stages), out_shap...  16.3 us
    unnamed x24, local copies, waits for them, and re-layouts  4.54 us

profile of v1, /device:TPU:1, one launch (start us, length us, event | category | flops | bytes accessed | tf_op | source)
XLA Modules:
  0.0 75.6 jit_solution(12473754477048814967)
XLA Ops:
  0.6 0.0 copy-start.1
  0.6 0.0 copy-start.3
  0.7 0.0 copy-start.4
  0.7 0.0 copy-start.5
  0.7 0.0 copy-start.6
  0.7 20.9 %relay_patches.1.patch_ref = f32[8,4,1024]{2,1,0:T(4,128)} custom-call(f32[32,4,256]{2,1,0:T(4,128)} %bitcast.6), custom_call_target="tpu_custom_call" | custom-call | tf_op jit(solution)/shard_map/relay_patches/pallas_call | solution.py:356
  21.6 0.0 copy-done.1
  21.6 0.0 copy-done.3
  21.6 0.0 copy-done.4
  21.6 0.0 copy-done.5
  21.6 0.0 copy-done.6
  21.6 0.0 copy-start
  21.6 0.9 %copy-done = f32[8,4,1024]{2,1,0:T(4,128)S(1)} copy-done((f32[8,4,1024]{2,1,0:T(4,128)S(1)}, f32[8,4,1024]{2,1,0:T(4,128)}, u32[]{:S(2)}) %copy-start) | copy-done | bytes 131096
  22.5 16.3 %train_patch.1 = (f32[32,1024]{1,0:T(8,128)}, f32[64,128]{1,0:T(8,128)S(1)}) custom-call(f32[8,4,1024]{2,1,0:T(4,128)S(1)} %copy-done, s32[32,1024]{1,0:T(8,128)S(1)} %bitcast.5, bf16[54,64]{1,0:T(8,128)(2,1)S(1)} %copy-done.4, f32[64]{0:T(128)S(1)} %copy-done.5, bf16[64,64]{1,0:T(8,128)(2,1)S(1)} %copy-done.3, f32[64]{0:T(128)S(1)} %copy-done.6), custom_call_target="tpu_custom_call" | custom-call | tf_op jit(solution)/shard_map/train_patch/pallas_call | solution.py:282
  38.8 0.0 copy-start.2
  38.8 0.6 copy-done.2
  39.4 33.1 %reduce_grads.1 = (f32[54,64]{1,0:T(8,128)}, f32[1,64]{1,0:T(1,128)}, f32[64,64]{1,0:T(8,128)}, f32[1,64]{1,0:T(1,128)}) custom-call(f32[64,128]{1,0:T(8,128)} %copy-done.2), custom_call_target="tpu_custom_call" | custom-call | tf_op jit(solution)/shard_map/reduce_grads/pallas_call | solution.py:414
  72.6 0.0 copy-start.7
  72.6 0.0 copy-start.9
  72.6 1.4 %copy.15 = f32[54,64]{1,0:T(8,128)} copy(f32[54,64]{1,0:T(8,128)} %get-tuple-element.23) | data formatting | bytes 27648
  74.0 0.0 copy-done.9
  74.0 0.5 copy.16
  74.5 0.0 copy-done.7
  74.5 0.0 copy-start.8
  74.5 0.6 copy.17
  75.1 0.0 copy-done.8
  75.1 0.5 copy.18
Async XLA Ops:
  0.6 20.9 %copy-start.1 = (s32[1,1,32,1024]{3,2,1,0:T(8,128)S(1)}, s32[1,1,32,1024]{3,2,1,0:T(8,128)}, u32[]{:S(2)}) copy-start(s32[1,1,32,1024]{3,2,1,0:T(8,128)} %param.7) | copy-start | bytes 393220
  0.6 20.9 %copy-start.3 = (bf16[64,64]{1,0:T(8,128)(2,1)S(1)}, bf16[64,64]{1,0:T(8,128)(2,1)}, u32[]{:S(2)}) copy-start(bf16[64,64]{1,0:T(8,128)(2,1)} %ow_ref.1) | copy-start | bytes 24580
  0.7 20.9 %copy-start.4 = (bf16[54,64]{1,0:T(8,128)(2,1)S(1)}, bf16[54,64]{1,0:T(8,128)(2,1)}, u32[]{:S(2)}) copy-start(bf16[54,64]{1,0:T(8,128)(2,1)} %cw_ref.1) | copy-start | bytes 20740
  0.7 20.9 %copy-start.5 = (f32[64]{0:T(128)S(1)}, f32[64]{0:T(128)}, u32[]{:S(2)}) copy-start(f32[64]{0:T(128)} %cb_ref.1) | copy-start | bytes 772
  0.7 20.9 %copy-start.6 = (f32[64]{0:T(128)S(1)}, f32[64]{0:T(128)}, u32[]{:S(2)}) copy-start(f32[64]{0:T(128)} %ob_ref.1) | copy-start | bytes 772
  21.6 0.9 %copy-start = (f32[8,4,1024]{2,1,0:T(4,128)S(1)}, f32[8,4,1024]{2,1,0:T(4,128)}, u32[]{:S(2)}) copy-start(f32[8,4,1024]{2,1,0:T(4,128)} %relay_patches.1.patch_ref) | copy-start | bytes 393220
  38.8 0.6 copy-start.2
  72.6 1.9 %copy-start.7 = (f32[64,64]{1,0:T(8,128)S(1)}, f32[64,64]{1,0:T(8,128)}, u32[]{:S(2)}) copy-start(f32[64,64]{1,0:T(8,128)} %get-tuple-element.25) | copy-start | bytes 49156
  72.6 1.4 %copy-start.9 = (f32[1,64]{1,0:T(1,128)S(1)}, f32[1,64]{1,0:T(1,128)}, u32[]{:S(2)}) copy-start(f32[1,64]{1,0:T(1,128)} %get-tuple-element.14) | copy-start | bytes 772
  74.5 0.6 copy-start.8

commit v2 on v1

--- a/solution.py
+++ b/solution.py
@@ -233,8 +233,7 @@
     ahead(jnp.minimum(step + 1, steps - 1), slot, c)
 
 
-def finish(z_ref, pick_ref, dconv_ref, dout_ref, hsum_ref, rsum_ref, loss_ref, part_ref):
-    loss_ref[...] = jnp.log(z_ref[...]) - pick_ref[...]
+def finish(dconv_ref, dout_ref, hsum_ref, rsum_ref, part_ref):
     total = dconv_ref[0:HID, :]
     for x in range(1, XB):
         total = total + pltpu.roll(dconv_ref[x * HID:(x + 1) * HID, :], KP - x, 1)
@@ -257,183 +256,245 @@
         pltpu.VMEM((XB * HID, KP), BF16), pltpu.VMEM((BINS, KO), BF16), pltpu.VMEM((HID, BINS), BF16),
         pltpu.VMEM((3, XB, HID, CH * TILE), BF16), pltpu.VMEM((3, XB, HID, CH * TILE), F32),
         pltpu.VMEM((2, XB, BINS, CH * TILE), BF16), pltpu.VMEM((2, XB * HID, CH * TILE), BF16),
-        pltpu.VMEM((PX, PLANE), F32), pltpu.VMEM((PX, PLANE), F32),
         pltpu.VMEM((XB * HID, KP), F32), pltpu.VMEM((HID, BINS), F32),
         pltpu.VMEM((HID, 128), F32), pltpu.VMEM((BINS, 128), F32),
     ]
 
 
-def compute_kernel(scale, stages, patch_ref, labels_ref, cw_ref, cb_ref, ow_ref, ob_ref, loss_ref, part_ref,
-                   pad, f0, f1, join, g, wide, owt, owb, act, d, low, grad, z, pick, dconv, dout, hsum, rsum):
-    if "p" in stages:
-        prepare(cw_ref, cb_ref, ow_ref, ob_ref, wide, owt, owb)
-    if "f" in stages:
-        filter_patch(patch_ref, pad, f0, f1)
-    if "s" in stages:
-        stencil(f0, f1, join, g)
-    if "t" in stages:
-        train(labels_ref, wide, owt, owb, g, act, d, low, grad, z, pick, dconv, dout, hsum, rsum, scale)
-    if "e" in stages:
-        finish(z, pick, dconv, dout, hsum, rsum, loss_ref, part_ref)
-
-
-def compute(patch, labels, cw, cb, ow, ob, scale, stages="pfste"):
-    vm = pl.BlockSpec(memory_space=pltpu.VMEM)
-    return pl.pallas_call(
-        functools.partial(compute_kernel, scale, stages),
-        out_shape=(jax.ShapeDtypeStruct((PX, PLANE), F32), jax.ShapeDtypeStruct((HID, 128), F32)),
-        in_specs=[vm] * 6,
-        out_specs=(vm, vm),
-        scratch_shapes=compute_scratch(),
-        compiler_params=pltpu.CompilerParams(vmem_limit_bytes=48 * 2**20),
-        name="train_patch",
-    )(patch, labels, cw, cb, ow, ob)
-
-
-SEC, SP, DP = 4, 8, 24
+SEC, SP, YHI, Z = 4, 8, 2, 12
 TEAM = SEC * SP
-PIECE = HID // TEAM
-
-
-def team_rank():
-    return lax.axis_index("sec") * SP + lax.axis_index("sp")
+Y = SEC * YHI
+ROWS = HID // SP
+SCALE = 1.0 / 25165824
+MESH = pl.DeviceIdType.MESH
+
+
+def place_here():
+    sec, sp, dp = lax.axis_index("sec"), lax.axis_index("sp"), lax.axis_index("dp")
+    return sec, sp, dp // Z, lax.rem(dp, Z)
 
 
 def team_device(rank):
-    return {"sec": rank // SP, "sp": rank % SP}
-
-
-def greet(team, replicas):
+    return {"sec": rank // SP, "sp": lax.rem(rank, SP)}
+
+
+def greet():
     barrier = pltpu.get_barrier_semaphore()
-    if team:
-        me = team_rank()
-
-        def hail(i, carry):
-            pl.semaphore_signal(barrier, inc=1, device_id=team_device(lax.rem(me + i, TEAM)), device_id_type=pl.DeviceIdType.MESH)
-            return carry
-
-        lax.fori_loop(1, TEAM, hail, 0)
-    if replicas:
-        mine = lax.axis_index("dp")
-
-        def call(i, carry):
-            pl.semaphore_signal(barrier, inc=1, device_id={"dp": lax.rem(mine + i, DP)}, device_id_type=pl.DeviceIdType.MESH)
-            return carry
-
-        lax.fori_loop(1, DP, call, 0)
-    pl.semaphore_wait(barrier, (TEAM - 1) * team + (DP - 1) * replicas)
-
-
-def relay_kernel(frac_ref, patch_ref, own_sem, send_sems, recv_sems):
-    greet(1, 0)
-    me = team_rank()
-    sec, sp = lax.axis_index("sec"), lax.axis_index("sp")
-    spot = patch_ref.at[sp, :, pl.ds(pl.multiple_of(sec * TILE, TILE), TILE)]
+    sec, sp, yhi, z = place_here()
+    me = sec * SP + sp
+
+    def hail(device):
+        pl.semaphore_signal(barrier, inc=1, device_id=device, device_id_type=MESH)
+
+    def along_z(i, carry):
+        hail({"dp": yhi * Z + lax.rem(z + i, Z)})
+        return carry
+
+    def along_y(i, carry):
+        hail({"sec": i, "dp": (1 - yhi) * Z + z})
+        return carry
+
+    def in_team(i, carry):
+        hail(team_device(lax.rem(me + i, TEAM)))
+        return carry
+
+    lax.fori_loop(1, Z, along_z, 0)
+    lax.fori_loop(0, SEC, along_y, 0)
+    lax.fori_loop(1, TEAM, in_team, 0)
+    pl.semaphore_wait(barrier, Z - 1 + SEC + TEAM - 1)
+
+
+def relay(frac_ref, patch_ref, own_sem, send_sems, recv_sems):
+    sec, sp, _, _ = place_here()
+    me = sec * SP + sp
+    spot = patch_ref.at[sp, :, pl.ds(pl.multiple_of(sec * (PLANE // SEC), PLANE // SEC), PLANE // SEC)]
 
     def parcel(rank, sender):
         return pltpu.make_async_remote_copy(
             src_ref=frac_ref.at[rank], dst_ref=spot, send_sem=send_sems.at[rank], recv_sem=recv_sems.at[sender],
-            device_id=team_device(rank), device_id_type=pl.DeviceIdType.MESH)
+            device_id=team_device(rank), device_id_type=MESH)
 
     def send(i, carry):
-        parcel(lax.rem(me + i, TEAM), me).start()
-        return carry
-
-    lax.fori_loop(1, TEAM, send, 0)
+        a, b = i // SP, lax.rem(i, SP)
+        far = jnp.where(sec < SEC // 2, SEC - 1 - a, a)
+        chip = lax.rem(sp // 2 + 2 + 3 * (b // 2), SP // 2)
+        rank = far * SP + chip * 2 + lax.rem(sp + b, 2)
+
+        @pl.when(rank != me)
+        def _():
+            parcel(rank, me).start()
+
+        return carry
+
+    lax.fori_loop(0, TEAM, send, 0)
     own = pltpu.make_async_copy(frac_ref.at[me], spot, own_sem)
     own.start()
 
-    def settle(i, carry):
-        other = lax.rem(me + i, TEAM)
-        parcel(other, other).wait()
-        return carry
-
-    lax.fori_loop(1, TEAM, settle, 0)
-    own.wait()
-
-
-def relay(frac):
-    return pl.pallas_call(
-        relay_kernel,
-        out_shape=jax.ShapeDtypeStruct((SP, 4, PLANE), F32),
-        in_specs=[pl.BlockSpec(memory_space=pl.ANY)],
-        out_specs=pl.BlockSpec(memory_space=pltpu.VMEM),
-        scratch_shapes=[pltpu.SemaphoreType.DMA, pltpu.SemaphoreType.DMA((TEAM,)), pltpu.SemaphoreType.DMA((TEAM,))],
-        compiler_params=pltpu.CompilerParams(collective_id=0, has_side_effects=True),
-        name="relay_patches",
-    )(frac)
-
-
-def swap(ref, slots, sends, recvs, count, me, device, source):
+    def arrive():
+        def take(i, carry):
+            other = lax.rem(me + i, TEAM)
+            parcel(other, other).wait_recv()
+            return carry
+
+        lax.fori_loop(1, TEAM, take, 0)
+        own.wait()
+
+    def leave():
+        def drop(i, carry):
+            other = lax.rem(me + i, TEAM)
+            parcel(other, other).wait_send()
+            return carry
+
+        lax.fori_loop(1, TEAM, drop, 0)
+
+    return arrive, leave
+
+
+def swap(count, me, device, source, slots, sends, recvs, meanwhile=None):
     def parcel(rank, sender):
         return pltpu.make_async_remote_copy(
             src_ref=source(rank), dst_ref=slots.at[sender], send_sem=sends.at[rank], recv_sem=recvs.at[sender],
-            device_id=device(rank), device_id_type=pl.DeviceIdType.MESH)
+            device_id=device(rank), device_id_type=MESH)
 
     def send(i, carry):
         parcel(lax.rem(me + i, count), me).start()
         return carry
 
+    def take(i, carry):
+        other = lax.rem(me + i, count)
+        parcel(other, other).wait_recv()
+        return carry
+
+    def leave():
+        def drop(i, carry):
+            other = lax.rem(me + i, count)
+            parcel(other, other).wait_send()
+            return carry
+
+        lax.fori_loop(1, count, drop, 0)
+
     lax.fori_loop(1, count, send, 0)
-
-    def settle(i, carry):
-        other = lax.rem(me + i, count)
-        parcel(other, other).wait()
-        return carry
-
-    lax.fori_loop(1, count, settle, 0)
-
-
-def reduce_kernel(part_ref, conv_ref, cbias_ref, out_ref, obias_ref, split, first, piece, second, total, result,
-                  s1, r1, s2, r2, s3, r3):
-    greet(1, 1)
-    me, mine = team_rank(), lax.axis_index("dp")
-    for j in range(TEAM):
-        split[j] = part_ref[PIECE * j:PIECE * (j + 1), :]
-    first[me] = split[me]
-    swap(None, first, s1, r1, TEAM, me, team_device, lambda rank: split.at[rank])
+    if meanwhile is not None:
+        meanwhile()
+    lax.fori_loop(1, count, take, 0)
+    return leave
+
+
+def reduce_grads(meanwhile, part, first, second, third, result, piece, piece2, total, s1, r1, s2, r2, s3, r3, s4, r4):
+    sec, sp, yhi, z = place_here()
+
+    def rows(rank):
+        return part.at[pl.ds(pl.multiple_of(rank * ROWS, ROWS), ROWS), :]
+
+    def own_chip(rank):
+        return {"sp": rank}
+
+    leaves = []
+    first[sp] = rows(sp)[...]
+    leaves.append(swap(SP, sp, own_chip, rows, first, s1, r1))
     piece[...] = jnp.sum(first[...], axis=0)
-    second[mine] = piece[...]
-    swap(None, second, s2, r2, DP, mine, lambda rank: {"dp": rank}, lambda rank: piece)
-    total[...] = jnp.sum(second[...], axis=0)
-    result[me] = total[...]
-    swap(None, result, s3, r3, TEAM, me, team_device, lambda rank: total)
-    for j in range(TEAM):
-        lo = PIECE * j
-        both = result[j]
-        out_ref[lo:lo + PIECE, :] = both[:, HID:]
-        if lo < FEATS:
-            conv_ref[lo:lo + PIECE, :] = both[:, :HID]
-        elif lo == FEATS:
-            cbias_ref[...] = both[0:1, :HID]
-            obias_ref[...] = both[1:2, :HID]
-
-
-def reduce_grads(part):
-    vm = pl.BlockSpec(memory_space=pltpu.VMEM)
+    y = yhi * SEC + sec
+    second[y] = piece[...]
+    leaves.append(swap(Y, y, lambda rank: {"sec": lax.rem(rank, SEC), "dp": rank // SEC * Z + z}, lambda rank: piece, second, s2, r2))
+    piece2[...] = jnp.sum(second[...], axis=0)
+    third[z] = piece2[...]
+    leaves.append(swap(Z, z, lambda rank: {"dp": yhi * Z + rank}, lambda rank: piece2, third, s3, r3, meanwhile))
+    total[...] = jnp.sum(third[...], axis=0)
+    result[sp] = total[...]
+    leaves.append(swap(SP, sp, own_chip, lambda rank: total, result, s4, r4))
+    return leaves
+
+
+def step_kernel(frac_ref, labels_ref, cw_ref, cb_ref, ow_ref, ob_ref, grads_ref, loss_ref,
+                z, pick, loss, out_sems, patch, labels, cw, cb, ow, ob, in_sems, own_sem, send_sems, recv_sems,
+                part, first, second, third, result, piece, piece2, total, s1, r1, s2, r2, s3, r3, s4, r4,
+                pad, f0, f1, join, g, wide, owt, owb, act, d, low, grad, dconv, dout, hsum, rsum):
+    loads = [pltpu.make_async_copy(src, dst, in_sems.at[i]) for i, (src, dst) in enumerate(
+        ((cw_ref, cw), (cb_ref, cb), (ow_ref, ow), (ob_ref, ob), (labels_ref, labels)))]
+    for load in loads:
+        load.start()
+    greet()
+    arrive, leave = relay(frac_ref, patch, own_sem, send_sems, recv_sems)
+    for load in loads:
+        load.wait()
+    prepare(cw, cb, ow, ob, wide, owt, owb)
+    arrive()
+    filter_patch(patch, pad, f0, f1)
+    stencil(f0, f1, join, g)
+    train(labels, wide, owt, owb, g, act, d, low, grad, z, pick, dconv, dout, hsum, rsum, SCALE)
+    finish(dconv, dout, hsum, rsum, part)
+
+    def save_loss():
+        loss[...] = jnp.log(z[...]) - pick[...]
+        pltpu.make_async_copy(loss, loss_ref, out_sems.at[0]).start()
+
+    leaves = reduce_grads(save_loss, part, first, second, third, result, piece, piece2, total, s1, r1, s2, r2, s3, r3, s4, r4)
+    save = pltpu.make_async_copy(result, grads_ref, out_sems.at[1])
+    save.start()
+    for end in [leave] + leaves:
+        end()
+    pltpu.make_async_copy(loss, loss_ref, out_sems.at[0]).wait()
+    save.wait()
+
+
+def train_step(frac, labels, cw, cb, ow, ob):
+    far = pl.BlockSpec(memory_space=pl.ANY)
+    dma = pltpu.SemaphoreType.DMA
+    tile = pltpu.VMEM((ROWS, 128), F32)
+    plane = pltpu.VMEM((PX, PLANE), F32)
     return pl.pallas_call(
-        reduce_kernel,
-        out_shape=(jax.ShapeDtypeStruct((FEATS, HID), F32), jax.ShapeDtypeStruct((1, HID), F32),
-                   jax.ShapeDtypeStruct((HID, BINS), F32), jax.ShapeDtypeStruct((1, BINS), F32)),
-        in_specs=[vm],
-        out_specs=(vm, vm, vm, vm),
+        step_kernel,
+        out_shape=(jax.ShapeDtypeStruct((SP, ROWS, 128), F32), jax.ShapeDtypeStruct((PX, PLANE), F32)),
+        in_specs=[far] * 6,
+        out_specs=(far, far),
         scratch_shapes=[
-            pltpu.VMEM((TEAM, PIECE, 128), F32), pltpu.VMEM((TEAM, PIECE, 128), F32), pltpu.VMEM((PIECE, 128), F32),
-            pltpu.VMEM((DP, PIECE, 128), F32), pltpu.VMEM((PIECE, 128), F32), pltpu.VMEM((TEAM, PIECE, 128), F32),
-            pltpu.SemaphoreType.DMA((TEAM,)), pltpu.SemaphoreType.DMA((TEAM,)),
-            pltpu.SemaphoreType.DMA((DP,)), pltpu.SemaphoreType.DMA((DP,)),
-            pltpu.SemaphoreType.DMA((TEAM,)), pltpu.SemaphoreType.DMA((TEAM,)),
-        ],
-        compiler_params=pltpu.CompilerParams(collective_id=1, has_side_effects=True),
-        name="reduce_grads",
-    )(part)
+            plane, plane, plane, dma((2,)),
+            pltpu.VMEM((SP, PX // SP, PLANE), F32), pltpu.VMEM((PX, PLANE), jnp.int32),
+            pltpu.VMEM((FEATS, HID), BF16), pltpu.VMEM((HID,), F32), pltpu.VMEM((HID, BINS), BF16), pltpu.VMEM((BINS,), F32),
+            dma((5,)), dma, dma((TEAM,)), dma((TEAM,)),
+            pltpu.VMEM((HID, 128), F32), pltpu.VMEM((SP, ROWS, 128), F32), pltpu.VMEM((Y, ROWS, 128), F32),
+            pltpu.VMEM((Z, ROWS, 128), F32), pltpu.VMEM((SP, ROWS, 128), F32), tile, tile, tile,
+            dma((SP,)), dma((SP,)), dma((Y,)), dma((Y,)), dma((Z,)), dma((Z,)), dma((SP,)), dma((SP,)),
+        ] + compute_scratch(),
+        compiler_params=pltpu.CompilerParams(collective_id=0, has_side_effects=True, vmem_limit_bytes=56 * 2**20),
+        name="train_step",
+    )(frac, labels, cw, cb, ow, ob)
+
+
+def close_kernel(grads_ref, loss_in, loss_ref, conv_ref, cbias_ref, out_ref, obias_ref, grads, sems):
+    loss = pltpu.make_async_copy(loss_in, loss_ref, sems.at[0])
+    load = pltpu.make_async_copy(grads_ref, grads, sems.at[1])
+    load.start()
+    loss.start()
+    load.wait()
+    full = jnp.concatenate([grads[i] for i in range(SP)], axis=0)
+    conv_ref[...] = full[:FEATS, :HID]
+    cbias_ref[...] = full[FEATS:FEATS + 1, :HID].reshape(HID)
+    obias_ref[...] = full[FEATS + 1:FEATS + 2, :HID].reshape(BINS)
+    out_ref[...] = full[:, HID:]
+    loss.wait()
+
+
+def close(grads, loss):
+    vm, far = pl.BlockSpec(memory_space=pltpu.VMEM), pl.BlockSpec(memory_space=pl.ANY)
+    return pl.pallas_call(
+        close_kernel,
+        out_shape=(jax.ShapeDtypeStruct((PX, PLANE), F32), jax.ShapeDtypeStruct((FEATS, HID), F32),
+                   jax.ShapeDtypeStruct((HID,), F32), jax.ShapeDtypeStruct((HID, BINS), F32),
+                   jax.ShapeDtypeStruct((BINS,), F32)),
+        in_specs=[far, far],
+        out_specs=(far, vm, vm, vm, vm),
+        scratch_shapes=[pltpu.VMEM((SP, ROWS, 128), F32), pltpu.SemaphoreType.DMA((2,))],
+        compiler_params=pltpu.CompilerParams(vmem_limit_bytes=56 * 2**20),
+        name="close_step",
+    )(grads, loss)
 
 
 def shards(fraction, labels, conv_weight, conv_bias, out_weight, out_bias):
-    patch = relay(fraction.reshape(fraction.shape[1:]))
-    loss, part = compute(patch, labels.reshape(PX, PLANE), conv_weight, conv_bias, out_weight, out_bias, 1.0 / 25165824)
-    conv, cbias, out, obias = reduce_grads(part)
-    return loss.reshape(labels.shape), conv, cbias.reshape(HID), out, obias.reshape(BINS)
+    grads, loss = train_step(fraction.reshape(fraction.shape[1:]), labels.reshape(PX, PLANE),
+                             conv_weight, conv_bias, out_weight, out_bias)
+    loss, conv, cbias, out, obias = close(grads, loss)
+    return loss.reshape(labels.shape), conv, cbias, out, obias
 
 
 def solution(mesh):

time: 75.9 us -> 67.4 us (0.89)
  local copies, waits for them, and re-layouts: 4.54 us -> 0 us
  Pallas kernels: 70.3 us -> 66.6 us
    unnamed x24 -> x0, local copies, waits for them, and re-layouts: 4.54 us -> none
    pallas_call x3 -> x2, Pallas kernels: 70.3 us -> 66.6 us  [the longest x1 60.9 us: train_step(): pl.pallas_call(step_kernel, out_shape=(jax.ShapeDtypeStruct((SP, ROWS, 12...]
where the time goes in v2:
time: 67.4 us; the launch traced here: 67.2 us
  Pallas kernels  66.6 us (99%)
    pallas_call x1, Pallas kernels, train_step(): pl.pallas_call(step_kernel, out_shape=(jax.ShapeDtypeStruct((SP, ROWS, 12...  60.9 us
    pallas_call x1, Pallas kernels, close(): pl.pallas_call(close_kernel, out_shape=(jax.ShapeDtypeStruct((PX, PLANE),...  5.72 us

profile of v2, /device:TPU:1, one launch (start us, length us, event | category | flops | bytes accessed | tf_op | source)
XLA Modules:
  0.0 67.2 jit_solution(9112272009884328600)
XLA Ops:
  0.6 60.9 %train_step.1 = (f32[8,8,128]{2,1,0:T(8,128)}, f32[32,1024]{1,0:T(8,128)}) custom-call(f32[32,4,256]{2,1,0:T(4,128)} %bitcast.3, s32[32,1024]{1,0:T(8,128)} %bitcast.4, bf16[54,64]{1,0:T(8,128)(2,1)} %cw_ref.1, f32[64]{0:T(128)} %cb_ref.1, bf16[64,64]{1,0:T(8,128)(2,1)} %ow_ref.1, f32[64]{0:T(128)} %ob_ref.1), custom_call_target="tpu_custom_call" | custom-call | tf_op jit(solution)/shard_map/train_step/pallas_call | solution.py:445
  61.5 5.7 %close_step.1 = (f32[32,1024]{1,0:T(8,128)}, f32[54,64]{1,0:T(8,128)}, f32[64]{0:T(128)}, f32[64,64]{1,0:T(8,128)}, f32[64]{0:T(128)}) custom-call(f32[8,8,128]{2,1,0:T(8,128)} %get-tuple-element.12.grads_ref, f32[32,1024]{1,0:T(8,128)} %get-tuple-element.13.loss_in), custom_call_target="tpu_custom_call" | custom-call | tf_op jit(solution)/shard_map/close_step/pallas_call | solution.py:480

commit v3 on v2

--- a/solution.py
+++ b/solution.py
@@ -19,8 +19,11 @@
 KO = HID + 16
 TILE = 256
 F32, BF16 = jnp.float32, jnp.bfloat16
-LEAD = 3
+LEAD = 2
 CH = 2
+HIDDEN_AT = (0, 6)
+CONV_AT = (1, 3)
+OUT_AT = (5, 7, 9, 11)
 NT = (((1,), (1,)), ((), ()))
 TN = (((0,), (0,)), ((), ()))
 
@@ -129,108 +132,128 @@
     return v[:, :128] + v[:, 128:]
 
 
-def train(labels_ref, wide_ref, owt_ref, owb_ref, g_ref, act_ref, d_ref, low_ref, grad_ref, z_ref, pick_ref, dconv_ref, dout_ref, hsum_ref, rsum_ref, scale):
-    dconv_ref[...] = jnp.zeros_like(dconv_ref)
-    dout_ref[...] = jnp.zeros_like(dout_ref)
-    hsum_ref[...] = jnp.zeros_like(hsum_ref)
-    rsum_ref[...] = jnp.zeros_like(rsum_ref)
-    low_ref[...] = jnp.zeros_like(low_ref)
-    grad_ref[...] = jnp.zeros_like(grad_ref)
-    act_ref[...] = jnp.zeros_like(act_ref)
-    bins = iota((BINS, TILE), 0)
+def train(labels_ref, bins_ref, early_ref, wide_ref, owt_ref, owb_ref, g_ref, act_ref, d_ref, low_ref, grad_ref, z_ref, pick_ref, dconv_ref, dout_ref, hsum_ref, rsum_ref, scale):
+    for ref in (dconv_ref, dout_ref, hsum_ref, rsum_ref, low_ref, grad_ref, act_ref, d_ref):
+        ref[...] = jnp.zeros_like(ref)
+    bins_ref[...] = iota((BINS, TILE), 0)
     ones = jnp.ones((16, TILE), BF16)
     width = CH * TILE
     per = PLANE // width
     steps = NB * per
+    tiles = [(c, x) for c in range(CH) for x in range(XB)]
+
+    def span(c):
+        return slice(c * TILE, (c + 1) * TILE)
 
     def place(step, c):
-        b = step // per
-        return b, pl.ds(pl.multiple_of((step % per) * width + c * TILE, TILE), TILE)
-
-    def whole(step):
-        b = step // per
-        return b, pl.ds(pl.multiple_of((step % per) * width, width), width)
-
-    def ahead(step, slot, c):
+        return step // per, pl.ds(pl.multiple_of((step % per) * width + c * TILE, TILE), TILE)
+
+    def within(step):
+        return jnp.clip(step, 0, steps - 1)
+
+    def hidden_dot(step, c):
+        b, cols = place(within(step), c)
+        return jnp.dot(wide_ref[...], g_ref[b, :, cols], preferred_element_type=F32)
+
+    def silu(step, c, x, u_all):
+        slot = lax.rem(step, 3)
+        u = u_all[x * HID:(x + 1) * HID]
+        t = jnp.tanh(u)
+        w = 1.0 + t
+        a = u * w
+        act_ref[slot, x, :, span(c)] = a.astype(BF16)
+        d_ref[slot, x, :, span(c)] = (w + a) - a * t
+
+    def hidden(step):
+        for c in range(CH):
+            u_all = hidden_dot(step, c)
+            for x in range(XB):
+                silu(step, c, x, u_all)
+
+    def logit(step, c, x):
+        slot = lax.rem(step, 3)
+        return jnp.dot(owt_ref[...], jnp.concatenate([act_ref[slot, x, :, span(c)], ones], axis=0), preferred_element_type=F32)
+
+    def softmax(step, c, x, logits):
         b, cols = place(step, c)
-        u_all = jnp.dot(wide_ref[...], g_ref[b, :, cols], preferred_element_type=F32)
-        for x in range(XB):
-            u = u_all[x * HID:(x + 1) * HID]
-            t = jnp.tanh(u)
-            w = 1.0 + t
-            a = u * w
-            act_ref[slot, x, :, c * TILE:(c + 1) * TILE] = a.astype(BF16)
-            d_ref[slot, x, :, c * TILE:(c + 1) * TILE] = (w + a) - a * t
-
-    def behind_out(step, act_slot, slot):
+        row = XB * b + x
+        e = jnp.exp(logits)
+        hot = jnp.where(bins_ref[...] == labels_ref[pl.ds(row, 1), cols], scale, 0.0)
+        picked = logits * hot
+        picked = sum(picked[8 * k:8 * k + 8] for k in range(BINS // 8))
+        for half in range(TILE // 128):
+            lane = (step % per) * (width // 128) + c * (TILE // 128) + half
+            pick_ref[lane, pl.ds(pl.multiple_of(8 * row, 8), 8), :] = picked[:, 128 * half:128 * half + 128]
+        total = jnp.sum(e, axis=0, keepdims=True)
+        z_ref[pl.ds(row, 1), cols] = total
+        r = e * (scale / total) - hot
+        low_ref[lax.rem(step, 2), x, :, span(c)] = r.astype(BF16)
+        return fold(r)
+
+    def back(step, c, x):
+        prod = jnp.dot(owb_ref[...], low_ref[lax.rem(step, 2), x, :, span(c)], preferred_element_type=F32)
+        grad = prod * d_ref[lax.rem(step, 3), x, :, span(c)]
+        grad_ref[lax.rem(step, 2), x * HID:(x + 1) * HID, span(c)] = grad.astype(BF16)
+        return fold(grad)
+
+    def out_grad(step, part, parts):
+        xs = range(part * XB // parts, (part + 1) * XB // parts)
         dout_ref[...] += lax.dot_general(
-            jnp.concatenate([act_ref[act_slot, x] for x in range(XB)], axis=1),
-            jnp.concatenate([low_ref[slot, x] for x in range(XB)], axis=1), NT, preferred_element_type=F32)
-
-    def behind_conv(step, slot):
-        b, cols = whole(step)
-        dconv_ref[...] += lax.dot_general(grad_ref[slot], g_ref[b, :, cols], NT, preferred_element_type=F32)
-
-    for c in range(CH):
-        ahead(0, 0, c)
+            jnp.concatenate([act_ref[lax.rem(step, 3), x] for x in xs], axis=1),
+            jnp.concatenate([low_ref[lax.rem(step, 2), x] for x in xs], axis=1), NT, preferred_element_type=F32)
+
+    def conv_grad(step, at, part, parts):
+        b = at // per
+        cols = pl.ds(pl.multiple_of((at % per) * width, width), width)
+        rows = slice(part * XB * HID // parts, (part + 1) * XB * HID // parts)
+        dconv_ref[rows, :] += lax.dot_general(grad_ref[lax.rem(step, 2), rows, :], g_ref[b, :, cols], NT, preferred_element_type=F32)
+
+    def add(total, term):
+        return term if total is None else total + term
+
+    hidden(0)
+    for i in range(LEAD):
+        early_ref[i] = logit(0, *tiles[i])
 
     def body(step, carry):
-        slot = lax.rem(step, 2)
-        slot3 = lax.rem(step, 3)
-        next3 = lax.rem(step + 1, 3)
-        last3 = lax.rem(step + 2, 3)
-        last = jnp.maximum(step - 1, 0)
-
-        def project(c, x):
-            return jnp.dot(owt_ref[...], jnp.concatenate([act_ref[slot3, x, :, c * TILE:(c + 1) * TILE], ones], axis=0), preferred_element_type=F32)
-
-        tiles = [(c, x) for c in range(CH) for x in range(XB)]
-        count = len(tiles)
-        logits_of = {i: project(*tiles[i]) for i in range(LEAD)}
-        backs = {}
+        old, oldest, ahead = step + 5, step + 4, step + 1
         hsum = rsum = None
-        for i in range(count + 1):
-            if i < count:
-                c, x = tiles[i]
-                span = slice(c * TILE, (c + 1) * TILE)
-                b, cols = place(step, c)
-                logits = logits_of.pop(i)
-                if i + LEAD < count:
-                    logits_of[i + LEAD] = project(*tiles[i + LEAD])
-                if i % XB == 0:
-                    ahead_at(ahead, step, next3, c, steps)
-                e = jnp.exp(logits)
-                row = XB * b + x
-                hit = bins == labels_ref[pl.ds(row, 1), cols]
-                total = jnp.sum(e, axis=0, keepdims=True)
-                z_ref[pl.ds(row, 1), cols] = total
-                pick_ref[pl.ds(row, 1), cols] = jnp.sum(jnp.where(hit, logits, 0.0), axis=0, keepdims=True)
-                r = e * (scale / total) - jnp.where(hit, scale, 0.0)
-                low = r.astype(BF16)
-                low_ref[slot, x, :, span] = low
-                rsum = fold(r) if rsum is None else rsum + fold(r)
-                backs[i] = jnp.dot(owb_ref[...], low, preferred_element_type=F32)
-                if i == count // 4:
-                    behind_out(last, last3, 1 - slot)
-                if i == count // 2:
-                    behind_conv(last, 1 - slot)
-            if i >= 1:
-                c, x = tiles[i - 1]
-                span = slice(c * TILE, (c + 1) * TILE)
-                grad = backs.pop(i - 1) * d_ref[slot3, x, :, span]
-                grad_ref[slot, x * HID:(x + 1) * HID, span] = grad.astype(BF16)
-                hsum = fold(grad) if hsum is None else hsum + fold(grad)
+        logits = {t: early_ref[i] for i, t in enumerate(tiles[:LEAD])}
+        n = len(tiles)
+        u_all = {}
+        for i, t in enumerate(tiles):
+            if i in HIDDEN_AT:
+                u_all[HIDDEN_AT.index(i)] = hidden_dot(ahead, HIDDEN_AT.index(i))
+            if i + LEAD < n:
+                logits[tiles[i + LEAD]] = logit(step, *tiles[i + LEAD])
+            if i in CONV_AT:
+                conv_grad(oldest, within(step - 2), CONV_AT.index(i), len(CONV_AT))
+            if i in OUT_AT:
+                out_grad(old, OUT_AT.index(i), len(OUT_AT))
+            hsum = add(hsum, back(old, *t))
+            silu(ahead, *t, u_all[t[0]])
+            rsum = add(rsum, softmax(step, *t, logits.pop(t)))
+        for i in range(LEAD):
+            early_ref[i] = logit(ahead, *tiles[i])
+        rsum_ref[...] += rsum
         hsum_ref[...] += hsum
-        rsum_ref[...] += rsum
         return carry
 
     lax.fori_loop(0, steps, body, 0)
-    behind_out(steps - 1, (steps - 1) % 3, (steps - 1) % 2)
-    behind_conv(steps - 1, (steps - 1) % 2)
-
-
-def ahead_at(ahead, step, slot, c, steps):
-    ahead(jnp.minimum(step + 1, steps - 1), slot, c)
+    hsum = None
+    for t in tiles:
+        hsum = add(hsum, back(steps - 1, *t))
+    hsum_ref[...] += hsum
+    conv_grad(steps - 2, steps - 2, 0, 1)
+    out_grad(steps - 1, 0, 1)
+    conv_grad(steps - 1, steps - 1, 0, 1)
+
+
+def losses(z_ref, pick_ref, loss_ref, scale):
+    for lane in range(PLANE // 128):
+        cols = slice(128 * lane, 128 * lane + 128)
+        picked = sum(pick_ref[lane, pl.ds(k, PX, stride=8), :] for k in range(8))
+        loss_ref[:, cols] = jnp.log(z_ref[:, cols]) - picked / scale
 
 
 def finish(dconv_ref, dout_ref, hsum_ref, rsum_ref, part_ref):
@@ -255,7 +278,7 @@
         pltpu.VMEM((NB, KP, PLANE), BF16),
         pltpu.VMEM((XB * HID, KP), BF16), pltpu.VMEM((BINS, KO), BF16), pltpu.VMEM((HID, BINS), BF16),
         pltpu.VMEM((3, XB, HID, CH * TILE), BF16), pltpu.VMEM((3, XB, HID, CH * TILE), F32),
-        pltpu.VMEM((2, XB, BINS, CH * TILE), BF16), pltpu.VMEM((2, XB * HID, CH * TILE), BF16),
+        pltpu.VMEM((2, XB, BINS, CH * TILE), BF16), pltpu.VMEM((2, XB * HID, CH * TILE), BF16), pltpu.VMEM((BINS, TILE), jnp.int32), pltpu.VMEM((LEAD, BINS, TILE), F32),
         pltpu.VMEM((XB * HID, KP), F32), pltpu.VMEM((HID, BINS), F32),
         pltpu.VMEM((HID, 128), F32), pltpu.VMEM((BINS, 128), F32),
     ]
@@ -408,7 +431,7 @@
 def step_kernel(frac_ref, labels_ref, cw_ref, cb_ref, ow_ref, ob_ref, grads_ref, loss_ref,
                 z, pick, loss, out_sems, patch, labels, cw, cb, ow, ob, in_sems, own_sem, send_sems, recv_sems,
                 part, first, second, third, result, piece, piece2, total, s1, r1, s2, r2, s3, r3, s4, r4,
-                pad, f0, f1, join, g, wide, owt, owb, act, d, low, grad, dconv, dout, hsum, rsum):
+                pad, f0, f1, join, g, wide, owt, owb, act, d, low, grad, bins, early, dconv, dout, hsum, rsum):
     loads = [pltpu.make_async_copy(src, dst, in_sems.at[i]) for i, (src, dst) in enumerate(
         ((cw_ref, cw), (cb_ref, cb), (ow_ref, ow), (ob_ref, ob), (labels_ref, labels)))]
     for load in loads:
@@ -421,11 +444,11 @@
     arrive()
     filter_patch(patch, pad, f0, f1)
     stencil(f0, f1, join, g)
-    train(labels, wide, owt, owb, g, act, d, low, grad, z, pick, dconv, dout, hsum, rsum, SCALE)
+    train(labels, bins, early, wide, owt, owb, g, act, d, low, grad, z, pick, dconv, dout, hsum, rsum, SCALE)
     finish(dconv, dout, hsum, rsum, part)
 
     def save_loss():
-        loss[...] = jnp.log(z[...]) - pick[...]
+        losses(z, pick, loss, SCALE)
         pltpu.make_async_copy(loss, loss_ref, out_sems.at[0]).start()
 
     leaves = reduce_grads(save_loss, part, first, second, third, result, piece, piece2, total, s1, r1, s2, r2, s3, r3, s4, r4)
@@ -448,7 +471,7 @@
         in_specs=[far] * 6,
         out_specs=(far, far),
         scratch_shapes=[
-            plane, plane, plane, dma((2,)),
+            plane, pltpu.VMEM((PLANE // 128, 8 * PX, 128), F32), plane, dma((2,)),
             pltpu.VMEM((SP, PX // SP, PLANE), F32), pltpu.VMEM((PX, PLANE), jnp.int32),
             pltpu.VMEM((FEATS, HID), BF16), pltpu.VMEM((HID,), F32), pltpu.VMEM((HID, BINS), BF16), pltpu.VMEM((BINS,), F32),
             dma((5,)), dma, dma((TEAM,)), dma((TEAM,)),
@@ -483,7 +506,7 @@
                    jax.ShapeDtypeStruct((HID,), F32), jax.ShapeDtypeStruct((HID, BINS), F32),
                    jax.ShapeDtypeStruct((BINS,), F32)),
         in_specs=[far, far],
-        out_specs=(far, vm, vm, vm, vm),
+        out_specs=(vm, vm, vm, vm, vm),
         scratch_shapes=[pltpu.VMEM((SP, ROWS, 128), F32), pltpu.SemaphoreType.DMA((2,))],
         compiler_params=pltpu.CompilerParams(vmem_limit_bytes=56 * 2**20),
         name="close_step",

time: 67.4 us -> 60.6 us (0.90)
  Pallas kernels: 66.6 us -> 59.8 us
    pallas_call x1, Pallas kernels: 5.72 us -> 1.62 us  [close(): pl.pallas_call(close_kernel, out_shape=(jax.ShapeDtypeStruct((PX, PLANE),...]
    pallas_call x1, Pallas kernels: 60.9 us -> 58.2 us  [train_step(): pl.pallas_call(step_kernel, out_shape=(jax.ShapeDtypeStruct((SP, ROWS, 12...]
where the time goes in v3:
time: 60.6 us; the launch traced here: 60.5 us
  Pallas kernels  59.8 us (99%)
  between operations  0.64 us (1%)
    pallas_call x1, Pallas kernels, train_step(): pl.pallas_call(step_kernel, out_shape=(jax.ShapeDtypeStruct((SP, ROWS, 12...  58.2 us
    pallas_call x1, Pallas kernels, close(): pl.pallas_call(close_kernel, out_shape=(jax.ShapeDtypeStruct((PX, PLANE),...  1.62 us

profile of v3, /device:TPU:1, one launch (start us, length us, event | category | flops | bytes accessed | tf_op | source)
XLA Modules:
  0.0 60.5 jit_solution(16829749654428982429)
XLA Ops:
  0.6 58.2 %train_step.1 = (f32[8,8,128]{2,1,0:T(8,128)}, f32[32,1024]{1,0:T(8,128)}) custom-call(f32[32,4,256]{2,1,0:T(4,128)} %bitcast.3, s32[32,1024]{1,0:T(8,128)} %bitcast.4, bf16[54,64]{1,0:T(8,128)(2,1)} %cw_ref.1, f32[64]{0:T(128)} %cb_ref.1, bf16[64,64]{1,0:T(8,128)(2,1)} %ow_ref.1, f32[64]{0:T(128)} %ob_ref.1), custom_call_target="tpu_custom_call" | custom-call | tf_op jit(solution)/shard_map/train_step/pallas_call | solution.py:468
  58.9 1.6 %close_step.1 = (f32[32,1024]{1,0:T(8,128)}, f32[54,64]{1,0:T(8,128)}, f32[64]{0:T(128)}, f32[64,64]{1,0:T(8,128)}, f32[64]{0:T(128)}) custom-call(f32[8,8,128]{2,1,0:T(8,128)} %get-tuple-element.12.grads_ref, f32[32,1024]{1,0:T(8,128)} %get-tuple-element.13.loss_in), custom_call_target="tpu_custom_call" | custom-call | tf_op jit(solution)/shard_map/close_step/pallas_call | solution.py:503

commit v4 on v3

--- a/solution.py
+++ b/solution.py
@@ -95,10 +95,6 @@
 
 
 def filter_patch(patch_ref, pad_ref, f0_ref, f1_ref):
-    zero = jnp.zeros((8, PLANE), F32)
-    for ref in (pad_ref, f0_ref, f1_ref):
-        ref[0:8, :] = zero
-        ref[40:48, :] = zero
     for i in range(8):
         pad_ref[8 + 4 * i:12 + 4 * i, :] = patch_ref[i]
     z_lo, z_hi, y_lo, y_hi = edges((PX, PLANE))
@@ -109,7 +105,6 @@
 
 def stencil(f0_ref, f1_ref, join_ref, g_ref):
     z_lo, z_hi, y_lo, y_hi = edges((GROUP, PLANE))
-    join_ref[20:24, :] = jnp.zeros((4, PLANE), F32)
     for b in range(NB):
         join_ref[0:10, :] = f0_ref[8 * b + 7:8 * b + 17, :]
         join_ref[10:20, :] = f1_ref[8 * b + 7:8 * b + 17, :]
@@ -132,10 +127,18 @@
     return v[:, :128] + v[:, 128:]
 
 
+def clear(bins_ref, d_ref, act_ref, low_ref, grad_ref, dconv_ref, dout_ref, hsum_ref, rsum_ref, pad_ref, f0_ref, f1_ref, join_ref):
+    bins_ref[...] = iota((BINS, TILE), 0)
+    for ref in (dconv_ref, dout_ref, hsum_ref, rsum_ref, grad_ref, d_ref.at[2], act_ref.at[2], low_ref.at[1]):
+        ref[...] = jnp.zeros(ref.shape, ref.dtype)
+    zero = jnp.zeros((8, PLANE), F32)
+    for ref in (pad_ref, f0_ref, f1_ref):
+        ref[0:8, :] = zero
+        ref[40:48, :] = zero
+    join_ref[20:24, :] = jnp.zeros((4, PLANE), F32)
+
+
 def train(labels_ref, bins_ref, early_ref, wide_ref, owt_ref, owb_ref, g_ref, act_ref, d_ref, low_ref, grad_ref, z_ref, pick_ref, dconv_ref, dout_ref, hsum_ref, rsum_ref, scale):
-    for ref in (dconv_ref, dout_ref, hsum_ref, rsum_ref, low_ref, grad_ref, act_ref, d_ref):
-        ref[...] = jnp.zeros_like(ref)
-    bins_ref[...] = iota((BINS, TILE), 0)
     ones = jnp.ones((16, TILE), BF16)
     width = CH * TILE
     per = PLANE // width
@@ -297,150 +300,114 @@
     return sec, sp, dp // Z, lax.rem(dp, Z)
 
 
-def team_device(rank):
-    return {"sec": rank // SP, "sp": lax.rem(rank, SP)}
-
-
-def greet():
+def flips(value):
+    return value, value + 1 - 2 * lax.rem(value, 2), lax.rem(value + 2, 4), 3 - value
+
+
+def sp_flips(sp):
+    chips, core = flips(sp // 2), lax.rem(sp, 2)
+    return [2 * chips[k // 2] + (1 - core if k % 2 else core) for k in range(SP)]
+
+
+CHIP_HOPS = (0, 1, 2, 1)
+SP_FAR = sorted(range(1, SP), key=lambda k: -CHIP_HOPS[k // 2])
+TEAM_FAR = sorted(((a, k) for a in range(SEC) for k in range(SP) if a or k), key=lambda t: -t[0] - CHIP_HOPS[t[1] // 2])
+Y_FAR = [(1, a) for a in (3, 2, 1, 0)] + [(0, a) for a in (3, 2, 1)]
+
+
+def rings():
+    sec, sp, yhi, z = place_here()
+    secs, sps = flips(sec), sp_flips(sp)
+    team = [(secs[a] * SP + sps[k], {"sec": secs[a], "sp": sps[k]}) for a, k in TEAM_FAR]
+    row = [(sps[k], {"sp": sps[k]}) for k in SP_FAR]
+    across = ((yhi, yhi * Z + z), (1 - yhi, (1 - yhi) * Z + z))
+    ys = [(across[f][0] * SEC + secs[a], {"sec": secs[a], "dp": across[f][1]}) for f, a in Y_FAR]
+    zs = []
+    for i in sorted(range(1, Z), key=lambda i: -min(i, Z - i)):
+        other = jnp.where(z + i >= Z, z + i - Z, z + i)
+        zs.append((other, {"dp": yhi * Z + other}))
+    return team, row, ys, zs
+
+
+def greet(*groups):
     barrier = pltpu.get_barrier_semaphore()
-    sec, sp, yhi, z = place_here()
-    me = sec * SP + sp
-
-    def hail(device):
-        pl.semaphore_signal(barrier, inc=1, device_id=device, device_id_type=MESH)
-
-    def along_z(i, carry):
-        hail({"dp": yhi * Z + lax.rem(z + i, Z)})
-        return carry
-
-    def along_y(i, carry):
-        hail({"sec": i, "dp": (1 - yhi) * Z + z})
-        return carry
-
-    def in_team(i, carry):
-        hail(team_device(lax.rem(me + i, TEAM)))
-        return carry
-
-    lax.fori_loop(1, Z, along_z, 0)
-    lax.fori_loop(0, SEC, along_y, 0)
-    lax.fori_loop(1, TEAM, in_team, 0)
-    pl.semaphore_wait(barrier, Z - 1 + SEC + TEAM - 1)
-
-
-def relay(frac_ref, patch_ref, own_sem, send_sems, recv_sems):
+    count = 0
+    for group in groups:
+        for _, device in group:
+            pl.semaphore_signal(barrier, inc=1, device_id=device, device_id_type=MESH)
+            count += 1
+    pl.semaphore_wait(barrier, count)
+
+
+def remote(src, dst, send_sem, recv_sem, device):
+    return pltpu.make_async_remote_copy(
+        src_ref=src, dst_ref=dst, send_sem=send_sem, recv_sem=recv_sem, device_id=device, device_id_type=MESH)
+
+
+def relay(team, frac_ref, patch_ref, send_sem, recv_sem):
     sec, sp, _, _ = place_here()
-    me = sec * SP + sp
     spot = patch_ref.at[sp, :, pl.ds(pl.multiple_of(sec * (PLANE // SEC), PLANE // SEC), PLANE // SEC)]
-
-    def parcel(rank, sender):
-        return pltpu.make_async_remote_copy(
-            src_ref=frac_ref.at[rank], dst_ref=spot, send_sem=send_sems.at[rank], recv_sem=recv_sems.at[sender],
-            device_id=team_device(rank), device_id_type=MESH)
-
-    def send(i, carry):
-        a, b = i // SP, lax.rem(i, SP)
-        far = jnp.where(sec < SEC // 2, SEC - 1 - a, a)
-        chip = lax.rem(sp // 2 + 2 + 3 * (b // 2), SP // 2)
-        rank = far * SP + chip * 2 + lax.rem(sp + b, 2)
-
-        @pl.when(rank != me)
-        def _():
-            parcel(rank, me).start()
-
-        return carry
-
-    lax.fori_loop(0, TEAM, send, 0)
-    own = pltpu.make_async_copy(frac_ref.at[me], spot, own_sem)
-    own.start()
+    for rank, device in team:
+        remote(frac_ref.at[rank], spot, send_sem, recv_sem, device).start()
+    pltpu.make_async_copy(frac_ref.at[sec * SP + sp], spot, recv_sem).start()
 
     def arrive():
-        def take(i, carry):
-            other = lax.rem(me + i, TEAM)
-            parcel(other, other).wait_recv()
-            return carry
-
-        lax.fori_loop(1, TEAM, take, 0)
-        own.wait()
+        pltpu.make_async_copy(patch_ref, patch_ref, recv_sem).wait()
 
     def leave():
-        def drop(i, carry):
-            other = lax.rem(me + i, TEAM)
-            parcel(other, other).wait_send()
-            return carry
-
-        lax.fori_loop(1, TEAM, drop, 0)
+        sent = frac_ref.at[pl.ds(0, TEAM - 1)]
+        remote(sent, sent, send_sem, recv_sem, team[0][1]).wait_send()
 
     return arrive, leave
 
 
-def swap(count, me, device, source, slots, sends, recvs, meanwhile=None):
-    def parcel(rank, sender):
-        return pltpu.make_async_remote_copy(
-            src_ref=source(rank), dst_ref=slots.at[sender], send_sem=sends.at[rank], recv_sem=recvs.at[sender],
-            device_id=device(rank), device_id_type=MESH)
-
-    def send(i, carry):
-        parcel(lax.rem(me + i, count), me).start()
-        return carry
-
-    def take(i, carry):
-        other = lax.rem(me + i, count)
-        parcel(other, other).wait_recv()
-        return carry
-
-    def leave():
-        def drop(i, carry):
-            other = lax.rem(me + i, count)
-            parcel(other, other).wait_send()
-            return carry
-
-        lax.fori_loop(1, count, drop, 0)
-
-    lax.fori_loop(1, count, send, 0)
+def swap(ring, me, source, slots, send_sem, recv_sem, meanwhile=None):
+    for rank, device in ring:
+        remote(source(rank), slots.at[me], send_sem, recv_sem, device).start()
     if meanwhile is not None:
         meanwhile()
-    lax.fori_loop(1, count, take, 0)
-    return leave
-
-
-def reduce_grads(meanwhile, part, first, second, third, result, piece, piece2, total, s1, r1, s2, r2, s3, r3, s4, r4):
+    others = slots.at[pl.ds(0, len(ring))]
+    both = remote(others, others, send_sem, recv_sem, ring[0][1])
+    both.wait_recv()
+    return both.wait_send
+
+
+def reduce_grads(meanwhile, row, ys, zs, part, first, second, third, result, piece, piece2, total, sends, recvs):
     sec, sp, yhi, z = place_here()
 
     def rows(rank):
         return part.at[pl.ds(pl.multiple_of(rank * ROWS, ROWS), ROWS), :]
 
-    def own_chip(rank):
-        return {"sp": rank}
-
-    leaves = []
     first[sp] = rows(sp)[...]
-    leaves.append(swap(SP, sp, own_chip, rows, first, s1, r1))
+    leaves = [swap(row, sp, rows, first, sends.at[0], recvs.at[0])]
     piece[...] = jnp.sum(first[...], axis=0)
     y = yhi * SEC + sec
     second[y] = piece[...]
-    leaves.append(swap(Y, y, lambda rank: {"sec": lax.rem(rank, SEC), "dp": rank // SEC * Z + z}, lambda rank: piece, second, s2, r2))
+    leaves.append(swap(ys, y, lambda rank: piece, second, sends.at[1], recvs.at[1]))
     piece2[...] = jnp.sum(second[...], axis=0)
     third[z] = piece2[...]
-    leaves.append(swap(Z, z, lambda rank: {"dp": yhi * Z + rank}, lambda rank: piece2, third, s3, r3, meanwhile))
+    leaves.append(swap(zs, z, lambda rank: piece2, third, sends.at[2], recvs.at[2], meanwhile))
     total[...] = jnp.sum(third[...], axis=0)
     result[sp] = total[...]
-    leaves.append(swap(SP, sp, own_chip, lambda rank: total, result, s4, r4))
+    leaves.append(swap(row, sp, lambda rank: total, result, sends.at[3], recvs.at[3]))
     return leaves
 
 
 def step_kernel(frac_ref, labels_ref, cw_ref, cb_ref, ow_ref, ob_ref, grads_ref, loss_ref,
-                z, pick, loss, out_sems, patch, labels, cw, cb, ow, ob, in_sems, own_sem, send_sems, recv_sems,
-                part, first, second, third, result, piece, piece2, total, s1, r1, s2, r2, s3, r3, s4, r4,
+                z, pick, loss, out_sems, patch, labels, cw, cb, ow, ob, in_sems, send_sems, recv_sems,
+                part, first, second, third, result, piece, piece2, total,
                 pad, f0, f1, join, g, wide, owt, owb, act, d, low, grad, bins, early, dconv, dout, hsum, rsum):
     loads = [pltpu.make_async_copy(src, dst, in_sems.at[i]) for i, (src, dst) in enumerate(
         ((cw_ref, cw), (cb_ref, cb), (ow_ref, ow), (ob_ref, ob), (labels_ref, labels)))]
     for load in loads:
         load.start()
-    greet()
-    arrive, leave = relay(frac_ref, patch, own_sem, send_sems, recv_sems)
+    team, row, ys, zs = rings()
+    greet(team, zs, ys[:SEC])
+    arrive, leave = relay(team, frac_ref, patch, send_sems.at[4], recv_sems.at[4])
     for load in loads:
         load.wait()
     prepare(cw, cb, ow, ob, wide, owt, owb)
+    clear(bins, d, act, low, grad, dconv, dout, hsum, rsum, pad, f0, f1, join)
     arrive()
     filter_patch(patch, pad, f0, f1)
     stencil(f0, f1, join, g)
@@ -451,7 +418,7 @@
         losses(z, pick, loss, SCALE)
         pltpu.make_async_copy(loss, loss_ref, out_sems.at[0]).start()
 
-    leaves = reduce_grads(save_loss, part, first, second, third, result, piece, piece2, total, s1, r1, s2, r2, s3, r3, s4, r4)
+    leaves = reduce_grads(save_loss, row, ys, zs, part, first, second, third, result, piece, piece2, total, send_sems, recv_sems)
     save = pltpu.make_async_copy(result, grads_ref, out_sems.at[1])
     save.start()
     for end in [leave] + leaves:
@@ -474,10 +441,9 @@
             plane, pltpu.VMEM((PLANE // 128, 8 * PX, 128), F32), plane, dma((2,)),
             pltpu.VMEM((SP, PX // SP, PLANE), F32), pltpu.VMEM((PX, PLANE), jnp.int32),
             pltpu.VMEM((FEATS, HID), BF16), pltpu.VMEM((HID,), F32), pltpu.VMEM((HID, BINS), BF16), pltpu.VMEM((BINS,), F32),
-            dma((5,)), dma, dma((TEAM,)), dma((TEAM,)),
+            dma((5,)), dma((5,)), dma((5,)),
             pltpu.VMEM((HID, 128), F32), pltpu.VMEM((SP, ROWS, 128), F32), pltpu.VMEM((Y, ROWS, 128), F32),
             pltpu.VMEM((Z, ROWS, 128), F32), pltpu.VMEM((SP, ROWS, 128), F32), tile, tile, tile,
-            dma((SP,)), dma((SP,)), dma((Y,)), dma((Y,)), dma((Z,)), dma((Z,)), dma((SP,)), dma((SP,)),
         ] + compute_scratch(),
         compiler_params=pltpu.CompilerParams(collective_id=0, has_side_effects=True, vmem_limit_bytes=56 * 2**20),
         name="train_step",

time: 60.6 us -> 59 us (0.974)
  Pallas kernels: 59.8 us -> 58.2 us
    pallas_call x1, Pallas kernels: 58.2 us -> 56.6 us  [train_step(): pl.pallas_call(step_kernel, out_shape=(jax.ShapeDtypeStruct((SP, ROWS, 12...]
where the time goes in v4:
time: 59 us; the launch traced here: 58.9 us
  Pallas kernels  58.2 us (99%)
  between operations  0.64 us (1%)
    pallas_call x1, Pallas kernels, train_step(): pl.pallas_call(step_kernel, out_shape=(jax.ShapeDtypeStruct((SP, ROWS, 12...  56.6 us
    pallas_call x1, Pallas kernels, close(): pl.pallas_call(close_kernel, out_shape=(jax.ShapeDtypeStruct((PX, PLANE),...  1.62 us

profile of v4, /device:TPU:1, one launch (start us, length us, event | category | flops | bytes accessed | tf_op | source)
XLA Modules:
  0.0 58.9 jit_solution(10891650258235415623)
XLA Ops:
  0.6 56.6 %train_step.1 = (f32[8,8,128]{2,1,0:T(8,128)}, f32[32,1024]{1,0:T(8,128)}) custom-call(f32[32,4,256]{2,1,0:T(4,128)} %bitcast.3, s32[32,1024]{1,0:T(8,128)} %bitcast.4, bf16[54,64]{1,0:T(8,128)(2,1)} %cw_ref.1, f32[64]{0:T(128)} %cb_ref.1, bf16[64,64]{1,0:T(8,128)(2,1)} %ow_ref.1, f32[64]{0:T(128)} %ob_ref.1), custom_call_target="tpu_custom_call" | custom-call | tf_op jit(solution)/shard_map/train_step/pallas_call | solution.py:435
  57.2 1.6 %close_step.1 = (f32[32,1024]{1,0:T(8,128)}, f32[54,64]{1,0:T(8,128)}, f32[64]{0:T(128)}, f32[64,64]{1,0:T(8,128)}, f32[64]{0:T(128)}) custom-call(f32[8,8,128]{2,1,0:T(8,128)} %get-tuple-element.12.grads_ref, f32[32,1024]{1,0:T(8,128)} %get-tuple-element.13.loss_in), custom_call_target="tpu_custom_call" | custom-call | tf_op jit(solution)/shard_map/close_step/pallas_call | solution.py:469

commit v5 on v4

--- a/solution.py
+++ b/solution.py
@@ -21,7 +21,7 @@
 F32, BF16 = jnp.float32, jnp.bfloat16
 LEAD = 2
 CH = 2
-HIDDEN_AT = (0, 6)
+HIDDEN_AT = (0, 4)
 CONV_AT = (1, 3)
 OUT_AT = (5, 7, 9, 11)
 NT = (((1,), (1,)), ((), ()))
@@ -77,64 +77,79 @@
     owb_ref[...] = (ow.astype(F32) * 0.5).astype(BF16)
 
 
-def box(padded_ref, square, z_lo, z_hi, y_lo, y_hi):
-    a, b, c = padded_ref[7:39, :], padded_ref[8:40, :], padded_ref[9:41, :]
-    if square:
-        s = a * a + b * b + c * c
-    else:
-        s = a + b + c
-    s = s + jnp.where(z_lo, 0.0, pltpu.roll(s, 1, 1)) + jnp.where(z_hi, 0.0, pltpu.roll(s, PLANE - 1, 1))
-    s = s + jnp.where(y_lo, 0.0, pltpu.roll(s, PZ, 1)) + jnp.where(y_hi, 0.0, pltpu.roll(s, PLANE - PZ, 1))
-    return s / 27.0
-
-
-def edges(shape):
-    pos = iota(shape, 1)
-    z = pos & (PZ - 1)
-    return z == 0, z == PZ - 1, pos < PZ, pos >= PLANE - PZ
-
-
-def filter_patch(patch_ref, pad_ref, f0_ref, f1_ref):
-    for i in range(8):
-        pad_ref[8 + 4 * i:12 + 4 * i, :] = patch_ref[i]
-    z_lo, z_hi, y_lo, y_hi = edges((PX, PLANE))
-    filt = box(pad_ref, False, z_lo, z_hi, y_lo, y_hi)
-    f0_ref[8:40, :] = filt
-    f1_ref[8:40, :] = box(pad_ref, True, z_lo, z_hi, y_lo, y_hi) - filt * filt
+def shift_z(parts, step):
+    z = iota(parts[0].shape, 1) & (PZ - 1)
+    edge = z == (0 if step > 0 else PZ - 1)
+    return [jnp.where(edge, 0.0, pltpu.roll(part, step % 128, 1)) for part in parts]
+
+
+def rows_wrap(step):
+    lane = iota((8, 128), 1)
+    return lane < PZ if step > 0 else lane >= 128 - PZ
+
+
+def shift_y(parts, step):
+    wraps = jnp.broadcast_to(rows_wrap(step)[0:1], parts[0].shape)
+    rolled = [pltpu.roll(part, step * PZ % 128, 1) for part in parts]
+    ends = [jnp.zeros_like(parts[0])]
+    near = ends + rolled[:-1] if step > 0 else rolled[1:] + ends
+    return [jnp.where(wraps, other, own) for other, own in zip(near, rolled)]
+
+
+def box(planes):
+    none = [jnp.zeros_like(planes[0])]
+    s = [a + b + c for a, b, c in zip(none + planes[:-1], planes, planes[1:] + none)]
+    s = [mid + lo + hi for mid, lo, hi in zip(s, shift_z(s, 1), shift_z(s, -1))]
+    group = iota((8, 128), 0)
+    sums = []
+    for v in s:
+        for step, last in ((1, 0), (-1, 7)):
+            rolled = pltpu.roll(v, step * PZ % 128, 1)
+            near = jnp.where(group == last, 0.0, pltpu.roll(rolled, step % 8, 0))
+            sums.append(jnp.where(rows_wrap(step), near, rolled))
+    return [(v + sums[2 * k] + sums[2 * k + 1]) / 27.0 for k, v in enumerate(s)]
+
+
+def filter_patch(patch_ref, f0_ref, f1_ref):
+    planes = [patch_ref[p // 4, pl.ds(p % 4, 8, stride=4), :] for p in range(PX)]
+    filt = box(planes)
+    square = box([p * p for p in planes])
+    for p in range(PX):
+        rows = slice(8 * p + 8, 8 * p + 16)
+        f0_ref[rows, :] = filt[p]
+        f1_ref[rows, :] = square[p] - filt[p] * filt[p]
 
 
 def stencil(f0_ref, f1_ref, join_ref, g_ref):
-    z_lo, z_hi, y_lo, y_hi = edges((GROUP, PLANE))
+    ones = jnp.ones((8, 128), F32)
     for b in range(NB):
-        join_ref[0:10, :] = f0_ref[8 * b + 7:8 * b + 17, :]
-        join_ref[10:20, :] = f1_ref[8 * b + 7:8 * b + 17, :]
-        mid = join_ref[...]
-        lo = jnp.where(z_lo, 0.0, pltpu.roll(mid, 1, 1))
-        hi = jnp.where(z_hi, 0.0, pltpu.roll(mid, PLANE - 1, 1))
-        parts = []
-        for step_y in (-1, 0, 1):
-            for v in (lo, mid, hi):
-                if step_y == -1:
-                    v = jnp.where(y_lo, 0.0, pltpu.roll(v, PZ, 1))
-                elif step_y == 1:
-                    v = jnp.where(y_hi, 0.0, pltpu.roll(v, PLANE - PZ, 1))
-                parts.append(v)
-        parts.append(jnp.ones((8, PLANE), F32))
-        g_ref[b] = jnp.concatenate(parts, axis=0).astype(BF16)
+        mid = []
+        for k in range(PLANE // 128):
+            cols = slice(128 * k, 128 * k + 128)
+            join_ref[0:10, cols] = f0_ref[pl.ds(64 * b + k, 10, stride=8), :]
+            join_ref[10:20, cols] = f1_ref[pl.ds(64 * b + k, 10, stride=8), :]
+            mid.append(join_ref[:, cols])
+        taps = []
+        for step_y in (1, 0, -1):
+            row = shift_y(mid, step_y) if step_y else mid
+            taps += [shift_z(row, 1), row, shift_z(row, -1)]
+        for k in range(PLANE // 128):
+            rows = jnp.concatenate([tap[k] for tap in taps] + [ones], axis=0)
+            g_ref[b, :, 128 * k:128 * k + 128] = rows.astype(BF16)
 
 
 def fold(v):
     return v[:, :128] + v[:, 128:]
 
 
-def clear(bins_ref, d_ref, act_ref, low_ref, grad_ref, dconv_ref, dout_ref, hsum_ref, rsum_ref, pad_ref, f0_ref, f1_ref, join_ref):
+def clear(bins_ref, d_ref, act_ref, low_ref, grad_ref, dconv_ref, dout_ref, hsum_ref, rsum_ref, f0_ref, f1_ref, join_ref):
     bins_ref[...] = iota((BINS, TILE), 0)
     for ref in (dconv_ref, dout_ref, hsum_ref, rsum_ref, grad_ref, d_ref.at[2], act_ref.at[2], low_ref.at[1]):
         ref[...] = jnp.zeros(ref.shape, ref.dtype)
-    zero = jnp.zeros((8, PLANE), F32)
-    for ref in (pad_ref, f0_ref, f1_ref):
+    zero = jnp.zeros((8, 128), F32)
+    for ref in (f0_ref, f1_ref):
         ref[0:8, :] = zero
-        ref[40:48, :] = zero
+        ref[8 * PX + 8:8 * PX + 16, :] = zero
     join_ref[20:24, :] = jnp.zeros((4, PLANE), F32)
 
 
@@ -227,13 +242,13 @@
         for i, t in enumerate(tiles):
             if i in HIDDEN_AT:
                 u_all[HIDDEN_AT.index(i)] = hidden_dot(ahead, HIDDEN_AT.index(i))
-            if i + LEAD < n:
-                logits[tiles[i + LEAD]] = logit(step, *tiles[i + LEAD])
+            hsum = add(hsum, back(old, *t))
             if i in CONV_AT:
                 conv_grad(oldest, within(step - 2), CONV_AT.index(i), len(CONV_AT))
             if i in OUT_AT:
                 out_grad(old, OUT_AT.index(i), len(OUT_AT))
-            hsum = add(hsum, back(old, *t))
+            if i + LEAD < n:
+                logits[tiles[i + LEAD]] = logit(step, *tiles[i + LEAD])
             silu(ahead, *t, u_all[t[0]])
             rsum = add(rsum, softmax(step, *t, logits.pop(t)))
         for i in range(LEAD):
@@ -247,9 +262,10 @@
     for t in tiles:
         hsum = add(hsum, back(steps - 1, *t))
     hsum_ref[...] += hsum
-    conv_grad(steps - 2, steps - 2, 0, 1)
+    for k in range(2):
+        conv_grad(steps - 1, steps - 1, k, 2)
+        conv_grad(steps - 2, steps - 2, k, 2)
     out_grad(steps - 1, 0, 1)
-    conv_grad(steps - 1, steps - 1, 0, 1)
 
 
 def losses(z_ref, pick_ref, loss_ref, scale):
@@ -276,7 +292,7 @@
 
 def compute_scratch():
     return [
-        pltpu.VMEM((48, PLANE), F32), pltpu.VMEM((48, PLANE), F32), pltpu.VMEM((48, PLANE), F32),
+        pltpu.VMEM((8 * PX + 16, 128), F32), pltpu.VMEM((8 * PX + 16, 128), F32),
         pltpu.VMEM((GROUP, PLANE), F32),
         pltpu.VMEM((NB, KP, PLANE), BF16),
         pltpu.VMEM((XB * HID, KP), BF16), pltpu.VMEM((BINS, KO), BF16), pltpu.VMEM((HID, BINS), BF16),
@@ -346,7 +362,7 @@
 
 def relay(team, frac_ref, patch_ref, send_sem, recv_sem):
     sec, sp, _, _ = place_here()
-    spot = patch_ref.at[sp, :, pl.ds(pl.multiple_of(sec * (PLANE // SEC), PLANE // SEC), PLANE // SEC)]
+    spot = patch_ref.at[sp, pl.ds(pl.multiple_of(8 * sec, 8), 8), :]
     for rank, device in team:
         remote(frac_ref.at[rank], spot, send_sem, recv_sem, device).start()
     pltpu.make_async_copy(frac_ref.at[sec * SP + sp], spot, recv_sem).start()
@@ -372,7 +388,7 @@
     return both.wait_send
 
 
-def reduce_grads(meanwhile, row, ys, zs, part, first, second, third, result, piece, piece2, total, sends, recvs):
+def reduce_grads(meanwhile, row, ys, zs, part, first, second, third, result_ref, piece, piece2, total, sends, recvs):
     sec, sp, yhi, z = place_here()
 
     def rows(rank):
@@ -388,15 +404,16 @@
     third[z] = piece2[...]
     leaves.append(swap(zs, z, lambda rank: piece2, third, sends.at[2], recvs.at[2], meanwhile))
     total[...] = jnp.sum(third[...], axis=0)
-    result[sp] = total[...]
-    leaves.append(swap(row, sp, lambda rank: total, result, sends.at[3], recvs.at[3]))
-    return leaves
+    mine = pltpu.make_async_copy(total, result_ref.at[sp], sends.at[5])
+    mine.start()
+    leaves.append(swap(row, sp, lambda rank: total, result_ref, sends.at[3], recvs.at[3]))
+    return leaves + [mine.wait]
 
 
 def step_kernel(frac_ref, labels_ref, cw_ref, cb_ref, ow_ref, ob_ref, grads_ref, loss_ref,
-                z, pick, loss, out_sems, patch, labels, cw, cb, ow, ob, in_sems, send_sems, recv_sems,
-                part, first, second, third, result, piece, piece2, total,
-                pad, f0, f1, join, g, wide, owt, owb, act, d, low, grad, bins, early, dconv, dout, hsum, rsum):
+                z, pick, loss, out_sem, patch, labels, cw, cb, ow, ob, in_sems, send_sems, recv_sems,
+                part, first, second, third, piece, piece2, total,
+                f0, f1, join, g, wide, owt, owb, act, d, low, grad, bins, early, dconv, dout, hsum, rsum):
     loads = [pltpu.make_async_copy(src, dst, in_sems.at[i]) for i, (src, dst) in enumerate(
         ((cw_ref, cw), (cb_ref, cb), (ow_ref, ow), (ob_ref, ob), (labels_ref, labels)))]
     for load in loads:
@@ -407,24 +424,21 @@
     for load in loads:
         load.wait()
     prepare(cw, cb, ow, ob, wide, owt, owb)
-    clear(bins, d, act, low, grad, dconv, dout, hsum, rsum, pad, f0, f1, join)
+    clear(bins, d, act, low, grad, dconv, dout, hsum, rsum, f0, f1, join)
     arrive()
-    filter_patch(patch, pad, f0, f1)
+    filter_patch(patch, f0, f1)
     stencil(f0, f1, join, g)
     train(labels, bins, early, wide, owt, owb, g, act, d, low, grad, z, pick, dconv, dout, hsum, rsum, SCALE)
     finish(dconv, dout, hsum, rsum, part)
 
     def save_loss():
         losses(z, pick, loss, SCALE)
-        pltpu.make_async_copy(loss, loss_ref, out_sems.at[0]).start()
-
-    leaves = reduce_grads(save_loss, row, ys, zs, part, first, second, third, result, piece, piece2, total, send_sems, recv_sems)
-    save = pltpu.make_async_copy(result, grads_ref, out_sems.at[1])
-    save.start()
+        pltpu.make_async_copy(loss, loss_ref, out_sem).start()
+
+    leaves = reduce_grads(save_loss, row, ys, zs, part, first, second, third, grads_ref, piece, piece2, total, send_sems, recv_sems)
     for end in [leave] + leaves:
         end()
-    pltpu.make_async_copy(loss, loss_ref, out_sems.at[0]).wait()
-    save.wait()
+    pltpu.make_async_copy(loss, loss_ref, out_sem).wait()
 
 
 def train_step(frac, labels, cw, cb, ow, ob):
@@ -438,12 +452,12 @@
         in_specs=[far] * 6,
         out_specs=(far, far),
         scratch_shapes=[
-            plane, pltpu.VMEM((PLANE // 128, 8 * PX, 128), F32), plane, dma((2,)),
-            pltpu.VMEM((SP, PX // SP, PLANE), F32), pltpu.VMEM((PX, PLANE), jnp.int32),
+            plane, pltpu.VMEM((PLANE // 128, 8 * PX, 128), F32), plane, dma,
+            pltpu.VMEM((SP, 8 * SEC, 128), F32), pltpu.VMEM((PX, PLANE), jnp.int32),
             pltpu.VMEM((FEATS, HID), BF16), pltpu.VMEM((HID,), F32), pltpu.VMEM((HID, BINS), BF16), pltpu.VMEM((BINS,), F32),
-            dma((5,)), dma((5,)), dma((5,)),
+            dma((5,)), dma((6,)), dma((5,)),
             pltpu.VMEM((HID, 128), F32), pltpu.VMEM((SP, ROWS, 128), F32), pltpu.VMEM((Y, ROWS, 128), F32),
-            pltpu.VMEM((Z, ROWS, 128), F32), pltpu.VMEM((SP, ROWS, 128), F32), tile, tile, tile,
+            pltpu.VMEM((Z, ROWS, 128), F32), tile, tile, tile,
         ] + compute_scratch(),
         compiler_params=pltpu.CompilerParams(collective_id=0, has_side_effects=True, vmem_limit_bytes=56 * 2**20),
         name="train_step",
@@ -480,7 +494,8 @@
 
 
 def shards(fraction, labels, conv_weight, conv_bias, out_weight, out_bias):
-    grads, loss = train_step(fraction.reshape(fraction.shape[1:]), labels.reshape(PX, PLANE),
+    blocks = fraction.reshape(TEAM, 4, 2, 128).transpose(0, 2, 1, 3).reshape(TEAM, 8, 128)
+    grads, loss = train_step(blocks, labels.reshape(PX, PLANE),
                              conv_weight, conv_bias, out_weight, out_bias)
     loss, conv, cbias, out, obias = close(grads, loss)
     return loss.reshape(labels.shape), conv, cbias, out, obias

time: 59 us -> 58.2 us (0.986)
  Pallas kernels: 58.2 us -> 57.4 us
    pallas_call x1, Pallas kernels: 56.6 us -> 55.8 us  [train_step(): pl.pallas_call(step_kernel, out_shape=(jax.ShapeDtypeStruct((SP, ROWS, 12...]
where the time goes in v5:
time: 58.2 us; the launch traced here: 58.1 us
  Pallas kernels  57.4 us (99%)
  between operations  0.64 us (1%)
    pallas_call x1, Pallas kernels, train_step(): pl.pallas_call(step_kernel, out_shape=(jax.ShapeDtypeStruct((SP, ROWS, 12...  55.8 us
    pallas_call x1, Pallas kernels, close(): pl.pallas_call(close_kernel, out_shape=(jax.ShapeDtypeStruct((PX, PLANE),...  1.62 us

profile of v5, /device:TPU:1, one launch (start us, length us, event | category | flops | bytes accessed | tf_op | source)
XLA Modules:
  0.0 58.1 jit_solution(13036921021866132444)
XLA Ops:
  0.6 55.8 %train_step.1 = (f32[8,8,128]{2,1,0:T(8,128)}, f32[32,1024]{1,0:T(8,128)}) custom-call(f32[32,8,128]{2,1,0:T(8,128)} %bitcast.7, s32[32,1024]{1,0:T(8,128)} %bitcast.8, bf16[54,64]{1,0:T(8,128)(2,1)} %cw_ref.1, f32[64]{0:T(128)} %cb_ref.1, bf16[64,64]{1,0:T(8,128)(2,1)} %ow_ref.1, f32[64]{0:T(128)} %ob_ref.1), custom_call_target="tpu_custom_call" | custom-call | tf_op jit(solution)/shard_map/train_step/pallas_call | solution.py:449
  56.4 1.6 %close_step.1 = (f32[32,1024]{1,0:T(8,128)}, f32[54,64]{1,0:T(8,128)}, f32[64]{0:T(128)}, f32[64,64]{1,0:T(8,128)}, f32[64]{0:T(128)}) custom-call(f32[8,8,128]{2,1,0:T(8,128)} %get-tuple-element.12.grads_ref, f32[32,1024]{1,0:T(8,128)} %get-tuple-element.13.loss_in), custom_call_target="tpu_custom_call" | custom-call | tf_op jit(solution)/shard_map/close_step/pallas_call | solution.py:483

commit v6 on v5

--- a/solution.py
+++ b/solution.py
@@ -142,8 +142,7 @@
     return v[:, :128] + v[:, 128:]
 
 
-def clear(bins_ref, d_ref, act_ref, low_ref, grad_ref, dconv_ref, dout_ref, hsum_ref, rsum_ref, f0_ref, f1_ref, join_ref):
-    bins_ref[...] = iota((BINS, TILE), 0)
+def clear(d_ref, act_ref, low_ref, grad_ref, dconv_ref, dout_ref, hsum_ref, rsum_ref, f0_ref, f1_ref, join_ref):
     for ref in (dconv_ref, dout_ref, hsum_ref, rsum_ref, grad_ref, d_ref.at[2], act_ref.at[2], low_ref.at[1]):
         ref[...] = jnp.zeros(ref.shape, ref.dtype)
     zero = jnp.zeros((8, 128), F32)
@@ -153,7 +152,19 @@
     join_ref[20:24, :] = jnp.zeros((4, PLANE), F32)
 
 
-def train(labels_ref, bins_ref, early_ref, wide_ref, owt_ref, owb_ref, g_ref, act_ref, d_ref, low_ref, grad_ref, z_ref, pick_ref, dconv_ref, dout_ref, hsum_ref, rsum_ref, scale):
+def mark(labels_ref, hot_ref, scale):
+    bins = iota((BINS, TILE), 0)
+
+    def body(row, carry):
+        for k in range(PLANE // TILE):
+            cols = slice(TILE * k, TILE * k + TILE)
+            hot_ref[row, :, cols] = jnp.where(bins == labels_ref[pl.ds(row, 1), cols], scale, 0.0)
+        return carry
+
+    lax.fori_loop(0, PX, body, 0)
+
+
+def train(hot_ref, early_ref, wide_ref, owt_ref, owb_ref, g_ref, act_ref, d_ref, low_ref, grad_ref, z_ref, pick_ref, dconv_ref, dout_ref, hsum_ref, rsum_ref, scale):
     ones = jnp.ones((16, TILE), BF16)
     width = CH * TILE
     per = PLANE // width
@@ -196,7 +207,7 @@
         b, cols = place(step, c)
         row = XB * b + x
         e = jnp.exp(logits)
-        hot = jnp.where(bins_ref[...] == labels_ref[pl.ds(row, 1), cols], scale, 0.0)
+        hot = hot_ref[row, :, cols]
         picked = logits * hot
         picked = sum(picked[8 * k:8 * k + 8] for k in range(BINS // 8))
         for half in range(TILE // 128):
@@ -297,7 +308,7 @@
         pltpu.VMEM((NB, KP, PLANE), BF16),
         pltpu.VMEM((XB * HID, KP), BF16), pltpu.VMEM((BINS, KO), BF16), pltpu.VMEM((HID, BINS), BF16),
         pltpu.VMEM((3, XB, HID, CH * TILE), BF16), pltpu.VMEM((3, XB, HID, CH * TILE), F32),
-        pltpu.VMEM((2, XB, BINS, CH * TILE), BF16), pltpu.VMEM((2, XB * HID, CH * TILE), BF16), pltpu.VMEM((BINS, TILE), jnp.int32), pltpu.VMEM((LEAD, BINS, TILE), F32),
+        pltpu.VMEM((2, XB, BINS, CH * TILE), BF16), pltpu.VMEM((2, XB * HID, CH * TILE), BF16), pltpu.VMEM((PX, BINS, PLANE), F32), pltpu.VMEM((LEAD, BINS, TILE), F32),
         pltpu.VMEM((XB * HID, KP), F32), pltpu.VMEM((HID, BINS), F32),
         pltpu.VMEM((HID, 128), F32), pltpu.VMEM((BINS, 128), F32),
     ]
@@ -377,65 +388,80 @@
     return arrive, leave
 
 
-def swap(ring, me, source, slots, send_sem, recv_sem, meanwhile=None):
+def post(ring, me, source, slots, send_sem, recv_sem):
     for rank, device in ring:
         remote(source(rank), slots.at[me], send_sem, recv_sem, device).start()
-    if meanwhile is not None:
-        meanwhile()
     others = slots.at[pl.ds(0, len(ring))]
     both = remote(others, others, send_sem, recv_sem, ring[0][1])
-    both.wait_recv()
-    return both.wait_send
-
-
-def reduce_grads(meanwhile, row, ys, zs, part, first, second, third, result_ref, piece, piece2, total, sends, recvs):
+    return both.wait_recv, both.wait_send
+
+
+def reduce_grads(meanwhile, row, ys, zs, part, first, yslots, zslots, pieces, total, result_ref, sends, recvs):
     sec, sp, yhi, z = place_here()
+    y = yhi * SEC + sec
+    half = ROWS // 2
+    leaves = []
 
     def rows(rank):
         return part.at[pl.ds(pl.multiple_of(rank * ROWS, ROWS), ROWS), :]
 
+    def share(ring, me, value, k, slots):
+        pieces[k] = value
+        slots[me] = value
+        take, leave = post(ring, me, lambda rank: pieces.at[k], slots, sends.at[k], recvs.at[k])
+        leaves.append(leave)
+        return take
+
     first[sp] = rows(sp)[...]
-    leaves = [swap(row, sp, rows, first, sends.at[0], recvs.at[0])]
-    piece[...] = jnp.sum(first[...], axis=0)
-    y = yhi * SEC + sec
-    second[y] = piece[...]
-    leaves.append(swap(ys, y, lambda rank: piece, second, sends.at[1], recvs.at[1]))
-    piece2[...] = jnp.sum(second[...], axis=0)
-    third[z] = piece2[...]
-    leaves.append(swap(zs, z, lambda rank: piece2, third, sends.at[2], recvs.at[2], meanwhile))
-    total[...] = jnp.sum(third[...], axis=0)
+    take, leave = post(row, sp, rows, first, sends.at[4], recvs.at[4])
+    leaves.append(leave)
+    take()
+    both = jnp.sum(first[...], axis=0)
+    take_z = share(zs, z, both[half:], 1, zslots.at[1])
+    take_y = share(ys, y, both[:half], 0, yslots.at[0])
+    take_y()
+    last_z = share(zs, z, jnp.sum(yslots[0], axis=0), 2, zslots.at[0])
+    take_z()
+    last_y = share(ys, y, jnp.sum(zslots[1], axis=0), 3, yslots.at[1])
+    meanwhile()
+    last_y()
+    total[half:, :] = jnp.sum(yslots[1], axis=0)
+    last_z()
+    total[:half, :] = jnp.sum(zslots[0], axis=0)
     mine = pltpu.make_async_copy(total, result_ref.at[sp], sends.at[5])
     mine.start()
-    leaves.append(swap(row, sp, lambda rank: total, result_ref, sends.at[3], recvs.at[3]))
-    return leaves + [mine.wait]
+    take, leave = post(row, sp, lambda rank: total, result_ref, sends.at[6], recvs.at[5])
+    take()
+    return leaves + [leave, mine.wait]
 
 
 def step_kernel(frac_ref, labels_ref, cw_ref, cb_ref, ow_ref, ob_ref, grads_ref, loss_ref,
                 z, pick, loss, out_sem, patch, labels, cw, cb, ow, ob, in_sems, send_sems, recv_sems,
-                part, first, second, third, piece, piece2, total,
-                f0, f1, join, g, wide, owt, owb, act, d, low, grad, bins, early, dconv, dout, hsum, rsum):
+                part, first, yslots, zslots, pieces, total,
+                f0, f1, join, g, wide, owt, owb, act, d, low, grad, hot, early, dconv, dout, hsum, rsum):
     loads = [pltpu.make_async_copy(src, dst, in_sems.at[i]) for i, (src, dst) in enumerate(
         ((cw_ref, cw), (cb_ref, cb), (ow_ref, ow), (ob_ref, ob), (labels_ref, labels)))]
     for load in loads:
         load.start()
     team, row, ys, zs = rings()
     greet(team, zs, ys[:SEC])
-    arrive, leave = relay(team, frac_ref, patch, send_sems.at[4], recv_sems.at[4])
+    arrive, leave = relay(team, frac_ref, patch, send_sems.at[7], recv_sems.at[6])
     for load in loads:
         load.wait()
     prepare(cw, cb, ow, ob, wide, owt, owb)
-    clear(bins, d, act, low, grad, dconv, dout, hsum, rsum, f0, f1, join)
+    clear(d, act, low, grad, dconv, dout, hsum, rsum, f0, f1, join)
+    mark(labels, hot, SCALE)
     arrive()
     filter_patch(patch, f0, f1)
     stencil(f0, f1, join, g)
-    train(labels, bins, early, wide, owt, owb, g, act, d, low, grad, z, pick, dconv, dout, hsum, rsum, SCALE)
+    train(hot, early, wide, owt, owb, g, act, d, low, grad, z, pick, dconv, dout, hsum, rsum, SCALE)
     finish(dconv, dout, hsum, rsum, part)
 
     def save_loss():
         losses(z, pick, loss, SCALE)
         pltpu.make_async_copy(loss, loss_ref, out_sem).start()
 
-    leaves = reduce_grads(save_loss, row, ys, zs, part, first, second, third, grads_ref, piece, piece2, total, send_sems, recv_sems)
+    leaves = reduce_grads(save_loss, row, ys, zs, part, first, yslots, zslots, pieces, total, grads_ref, send_sems, recv_sems)
     for end in [leave] + leaves:
         end()
     pltpu.make_async_copy(loss, loss_ref, out_sem).wait()
@@ -444,7 +470,6 @@
 def train_step(frac, labels, cw, cb, ow, ob):
     far = pl.BlockSpec(memory_space=pl.ANY)
     dma = pltpu.SemaphoreType.DMA
-    tile = pltpu.VMEM((ROWS, 128), F32)
     plane = pltpu.VMEM((PX, PLANE), F32)
     return pl.pallas_call(
         step_kernel,
@@ -455,9 +480,9 @@
             plane, pltpu.VMEM((PLANE // 128, 8 * PX, 128), F32), plane, dma,
             pltpu.VMEM((SP, 8 * SEC, 128), F32), pltpu.VMEM((PX, PLANE), jnp.int32),
             pltpu.VMEM((FEATS, HID), BF16), pltpu.VMEM((HID,), F32), pltpu.VMEM((HID, BINS), BF16), pltpu.VMEM((BINS,), F32),
-            dma((5,)), dma((6,)), dma((5,)),
-            pltpu.VMEM((HID, 128), F32), pltpu.VMEM((SP, ROWS, 128), F32), pltpu.VMEM((Y, ROWS, 128), F32),
-            pltpu.VMEM((Z, ROWS, 128), F32), tile, tile, tile,
+            dma((5,)), dma((8,)), dma((7,)),
+            pltpu.VMEM((HID, 128), F32), pltpu.VMEM((SP, ROWS, 128), F32), pltpu.VMEM((2, Y, ROWS // 2, 128), F32),
+            pltpu.VMEM((2, Z, ROWS // 2, 128), F32), pltpu.VMEM((4, ROWS // 2, 128), F32), pltpu.VMEM((ROWS, 128), F32),
         ] + compute_scratch(),
         compiler_params=pltpu.CompilerParams(collective_id=0, has_side_effects=True, vmem_limit_bytes=56 * 2**20),
         name="train_step",

time: 58.2 us -> 58 us (level)
  no operation moved by 1% of the time
where the time goes in v6:
time: 58 us; the launch traced here: 57.8 us
  Pallas kernels  57.2 us (99%)
  between operations  0.64 us (1%)
    pallas_call x1, Pallas kernels, train_step(): pl.pallas_call(step_kernel, out_shape=(jax.ShapeDtypeStruct((SP, ROWS, 12...  55.6 us
    pallas_call x1, Pallas kernels, close(): pl.pallas_call(close_kernel, out_shape=(jax.ShapeDtypeStruct((PX, PLANE),...  1.62 us

profile of v6, /device:TPU:1, one launch (start us, length us, event | category | flops | bytes accessed | tf_op | source)
XLA Modules:
  0.0 57.8 jit_solution(17330192568913415204)
XLA Ops:
  0.6 55.6 %train_step.1 = (f32[8,8,128]{2,1,0:T(8,128)}, f32[32,1024]{1,0:T(8,128)}) custom-call(f32[32,8,128]{2,1,0:T(8,128)} %bitcast.7, s32[32,1024]{1,0:T(8,128)} %bitcast.8, bf16[54,64]{1,0:T(8,128)(2,1)} %cw_ref.1, f32[64]{0:T(128)} %cb_ref.1, bf16[64,64]{1,0:T(8,128)(2,1)} %ow_ref.1, f32[64]{0:T(128)} %ob_ref.1), custom_call_target="tpu_custom_call" | custom-call | tf_op jit(solution)/shard_map/train_step/pallas_call | solution.py:474
  56.2 1.6 %close_step.1 = (f32[32,1024]{1,0:T(8,128)}, f32[54,64]{1,0:T(8,128)}, f32[64]{0:T(128)}, f32[64,64]{1,0:T(8,128)}, f32[64]{0:T(128)}) custom-call(f32[8,8,128]{2,1,0:T(8,128)} %get-tuple-element.12.grads_ref, f32[32,1024]{1,0:T(8,128)} %get-tuple-element.13.loss_in), custom_call_target="tpu_custom_call" | custom-call | tf_op jit(solution)/shard_map/close_step/pallas_call | solution.py:508

commit v7 on v6

--- a/solution.py
+++ b/solution.py
@@ -283,7 +283,7 @@
     for lane in range(PLANE // 128):
         cols = slice(128 * lane, 128 * lane + 128)
         picked = sum(pick_ref[lane, pl.ds(k, PX, stride=8), :] for k in range(8))
-        loss_ref[:, cols] = jnp.log(z_ref[:, cols]) - picked / scale
+        loss_ref[:, cols] = jnp.log(z_ref[0:PX, cols]) - picked / scale
 
 
 def finish(dconv_ref, dout_ref, hsum_ref, rsum_ref, part_ref):
@@ -303,7 +303,7 @@
 
 def compute_scratch():
     return [
-        pltpu.VMEM((8 * PX + 16, 128), F32), pltpu.VMEM((8 * PX + 16, 128), F32),
+        pltpu.VMEM((8 * PX + 80, 128), F32), pltpu.VMEM((8 * PX + 80, 128), F32),
         pltpu.VMEM((GROUP, PLANE), F32),
         pltpu.VMEM((NB, KP, PLANE), BF16),
         pltpu.VMEM((XB * HID, KP), BF16), pltpu.VMEM((BINS, KO), BF16), pltpu.VMEM((HID, BINS), BF16),
@@ -356,13 +356,15 @@
     return team, row, ys, zs
 
 
-def greet(*groups):
+def greet(loads, *groups):
     barrier = pltpu.get_barrier_semaphore()
     count = 0
     for group in groups:
         for _, device in group:
             pl.semaphore_signal(barrier, inc=1, device_id=device, device_id_type=MESH)
             count += 1
+    for load in loads:
+        load.start()
     pl.semaphore_wait(barrier, count)
 
 
@@ -440,11 +442,9 @@
                 part, first, yslots, zslots, pieces, total,
                 f0, f1, join, g, wide, owt, owb, act, d, low, grad, hot, early, dconv, dout, hsum, rsum):
     loads = [pltpu.make_async_copy(src, dst, in_sems.at[i]) for i, (src, dst) in enumerate(
-        ((cw_ref, cw), (cb_ref, cb), (ow_ref, ow), (ob_ref, ob), (labels_ref, labels)))]
-    for load in loads:
-        load.start()
+        ((cw_ref, cw), (cb_ref, cb), (ow_ref, ow), (ob_ref, ob), (labels_ref, labels.at[pl.ds(0, PX)])))]
     team, row, ys, zs = rings()
-    greet(team, zs, ys[:SEC])
+    greet(loads, team, zs, ys[:SEC])
     arrive, leave = relay(team, frac_ref, patch, send_sems.at[7], recv_sems.at[6])
     for load in loads:
         load.wait()
@@ -470,15 +470,14 @@
 def train_step(frac, labels, cw, cb, ow, ob):
     far = pl.BlockSpec(memory_space=pl.ANY)
     dma = pltpu.SemaphoreType.DMA
-    plane = pltpu.VMEM((PX, PLANE), F32)
     return pl.pallas_call(
         step_kernel,
         out_shape=(jax.ShapeDtypeStruct((SP, ROWS, 128), F32), jax.ShapeDtypeStruct((PX, PLANE), F32)),
         in_specs=[far] * 6,
         out_specs=(far, far),
         scratch_shapes=[
-            plane, pltpu.VMEM((PLANE // 128, 8 * PX, 128), F32), plane, dma,
-            pltpu.VMEM((SP, 8 * SEC, 128), F32), pltpu.VMEM((PX, PLANE), jnp.int32),
+            pltpu.VMEM((PX + 8, PLANE), F32), pltpu.VMEM((PLANE // 128, 8 * PX, 128), F32), pltpu.VMEM((PX, PLANE), F32), dma,
+            pltpu.VMEM((SP, 8 * SEC, 128), F32), pltpu.VMEM((PX + 8, PLANE), jnp.int32),
             pltpu.VMEM((FEATS, HID), BF16), pltpu.VMEM((HID,), F32), pltpu.VMEM((HID, BINS), BF16), pltpu.VMEM((BINS,), F32),
             dma((5,)), dma((8,)), dma((7,)),
             pltpu.VMEM((HID, 128), F32), pltpu.VMEM((SP, ROWS, 128), F32), pltpu.VMEM((2, Y, ROWS // 2, 128), F32),

time: 58 us -> 58 us (level)
  no operation moved by 1% of the time
where the time goes in v7:
time: 58 us; the launch traced here: 57.8 us
  Pallas kernels  57.2 us (99%)
  between operations  0.64 us (1%)
    pallas_call x1, Pallas kernels, train_step(): pl.pallas_call(step_kernel, out_shape=(jax.ShapeDtypeStruct((SP, ROWS, 12...  55.6 us
    pallas_call x1, Pallas kernels, close(): pl.pallas_call(close_kernel, out_shape=(jax.ShapeDtypeStruct((PX, PLANE),...  1.62 us

profile of v7, /device:TPU:1, one launch (start us, length us, event | category | flops | bytes accessed | tf_op | source)
XLA Modules:
  0.0 57.8 jit_solution(7180974704004804535)
XLA Ops:
  0.6 55.6 %train_step.1 = (f32[8,8,128]{2,1,0:T(8,128)}, f32[32,1024]{1,0:T(8,128)}) custom-call(f32[32,8,128]{2,1,0:T(8,128)} %bitcast.7, s32[32,1024]{1,0:T(8,128)} %bitcast.8, bf16[54,64]{1,0:T(8,128)(2,1)} %cw_ref.1, f32[64]{0:T(128)} %cb_ref.1, bf16[64,64]{1,0:T(8,128)(2,1)} %ow_ref.1, f32[64]{0:T(128)} %ob_ref.1), custom_call_target="tpu_custom_call" | custom-call | tf_op jit(solution)/shard_map/train_step/pallas_call | solution.py:473
  56.2 1.6 %close_step.1 = (f32[32,1024]{1,0:T(8,128)}, f32[54,64]{1,0:T(8,128)}, f32[64]{0:T(128)}, f32[64,64]{1,0:T(8,128)}, f32[64]{0:T(128)}) custom-call(f32[8,8,128]{2,1,0:T(8,128)} %get-tuple-element.12.grads_ref, f32[32,1024]{1,0:T(8,128)} %get-tuple-element.13.loss_in), custom_call_target="tpu_custom_call" | custom-call | tf_op jit(solution)/shard_map/close_step/pallas_call | solution.py:507
